TPU v7x, 512 devices: a whole 4x4x16 slice. The times are simulated.
512 devices in a mesh: helix: 32 (over z_lo, y), cross: 4 (over x), cls: 4 (over z_hi, core).
Axes of the slice: x: 4, y: 4, z: 16 (z_hi: 2, z_lo: 8; z = z_hi * 8 + z_lo), core: 2. Of those that a mesh axis runs over, the one named last changes fastest.
Arguments:
- concentration: float32 [64, 1024, 4096], P('cls', 'helix', 'cross'), may hold values from 0 to 0.9, as said below
- class_table: int32 [64], P('cls'), may hold values from 0 to 63, as said below
- settle_speed: float32 [64], replicated, may hold values from 0.05 to 2
- along_speed: float32 [1024, 4096], P('helix', 'cross'), may hold values from 0.2 to 1
- across_speed: float32 [1024, 4096], P('helix', 'cross'), may hold values from -0.5 to 0.5
- film_depth: float32 [1024, 4096], P('helix', 'cross'), may hold values from 0.5 to 2
- cell_mask: int32 [1024, 4096], P('helix', 'cross'), may hold values from 0 to 2
Outputs:
- advanced: float32 [64, 1024, 4096], P('cls', 'helix', 'cross')
Inputs may be any that keep to these rules, and one draw needn't show every extreme that they name: `concentration`: every entry is nonnegative, and the sum over all 64 slots of a cell stays below 58. `class_table`: each class 0 .. 63 is held in exactly one slot.
All inputs are finite; a program needn't handle non-finite values.
Results may differ from a plain program's by a relative error of at most 0.00002.
Values sent between devices are 32-bit elements; how exact they have to be, the bound alone decides.
A program may use at most 64 MiB of HBM per device.

v0:
```python
import jax
import jax.numpy as jnp
from jax import lax
from jax.sharding import PartitionSpec as P

TIME_STEP = 0.25
DIFFUSION = 0.1
VOLUME_PER_UNIT = 0.01
EXPONENT = 4.65


def padded(cells, sides, width, closed):
    for axis, dim in sides:
        count = lax.axis_size(axis)
        ends = count if closed else count - 1
        head = lax.slice_in_dim(cells, 0, width, axis=dim)
        tail = lax.slice_in_dim(cells, cells.shape[dim] - width, cells.shape[dim], axis=dim)
        cells = jnp.concatenate(
            [
                lax.ppermute(tail, axis, [(i, (i + 1) % count) for i in range(ends)]),
                cells,
                lax.ppermute(head, axis, [((i + 1) % count, i) for i in range(ends)]),
            ],
            axis=dim,
        )
    return cells


def tendency(extended, speeds, hindrance):
    local_classes = speeds.shape[0]
    fields = extended[:local_classes]
    along = extended[local_classes]
    across = extended[local_classes + 1]
    wetted = extended[local_classes + 2]
    bed_rate = extended[local_classes + 3]
    lower_cells = fields[:, :-1, 1:-1]
    upper_cells = fields[:, 1:, 1:-1]
    face_speed = 0.5 * (along[:-1, 1:-1] + along[1:, 1:-1])
    opening = wetted[:-1, 1:-1] * wetted[1:, 1:-1]
    flux_rows = opening * (
        jnp.maximum(face_speed, 0.0) * lower_cells
        + jnp.minimum(face_speed, 0.0) * upper_cells
        - DIFFUSION * (upper_cells - lower_cells)
    )
    divergence = flux_rows[:, 1:] - flux_rows[:, :-1]
    lower_cells = fields[:, 1:-1, :-1]
    upper_cells = fields[:, 1:-1, 1:]
    face_speed = 0.5 * (across[1:-1, :-1] + across[1:-1, 1:])
    opening = wetted[1:-1, :-1] * wetted[1:-1, 1:]
    flux_cols = opening * (
        jnp.maximum(face_speed, 0.0) * lower_cells
        + jnp.minimum(face_speed, 0.0) * upper_cells
        - DIFFUSION * (upper_cells - lower_cells)
    )
    divergence = divergence + flux_cols[:, :, 1:] - flux_cols[:, :, :-1]
    centre = fields[:, 1:-1, 1:-1]
    settle = speeds[:, None, None] * (hindrance * bed_rate[1:-1, 1:-1])[None] * centre
    return -divergence - settle


def hindered(partial_solids):
    solids = lax.psum(partial_solids, "cls")
    return (1.0 - VOLUME_PER_UNIT * solids) ** EXPONENT


def per_device(
    concentration, class_table, settle_speed, along_speed, across_speed, film_depth, cell_mask
):
    matches = class_table[:, None] == jnp.arange(settle_speed.shape[0], dtype=jnp.int32)[None, :]
    slot_speed = jnp.sum(jnp.where(matches, settle_speed[None, :], 0.0), axis=1)
    wetted = (cell_mask > 0).astype(jnp.float32)
    bed_rate = (cell_mask == 2).astype(jnp.float32) / film_depth
    static = jnp.stack([along_speed, across_speed, wetted, bed_rate])

    def extend(fields):
        stacked = jnp.concatenate([fields, static], axis=0)
        row_ext = padded(stacked, (("helix", 1),), 1, True)
        return padded(row_ext, (("cross", 2),), 1, False)

    hindrance = hindered(jnp.sum(concentration, axis=0))
    section_one = concentration + TIME_STEP * tendency(extend(concentration), slot_speed, hindrance)
    hindrance = hindered(jnp.sum(section_one, axis=0))
    section_two = section_one + TIME_STEP * tendency(extend(section_one), slot_speed, hindrance)
    return 0.5 * concentration + 0.5 * section_two


def solution(mesh):
    placed = (
        P("cls", "helix", "cross"),
        P("cls"),
        P(),
        P("helix", "cross"),
        P("helix", "cross"),
        P("helix", "cross"),
        P("helix", "cross"),
    )
    return jax.shard_map(
        per_device,
        mesh=mesh,
        in_specs=placed,
        out_specs=P("cls", "helix", "cross"),
        check_vma=False,
    )
```

profile of v0, /device:TPU:1, one launch (start us, length us, event | category | flops | bytes accessed | tf_op | source)
XLA Modules:
  0.0 235.7 jit_solution(18292621619188500538)
XLA Ops:
  6.6 2.6 %fusion.20 = (f32[32,1024]{1,0:T(8,128)}, f32[20,32,1024]{2,1,0:T(8,128)S(1)}) fusion(f32[16,32,1024]{2,1,0:T(8,128)} %param.7), kind=kLoop, calls=%fused_computation.87 | loop fusion | flops 491519 | bytes 4325376 | tf_op jit(solution)/shard_map/reduce_sum | solution.py:80
  9.4 4.0 %collective-permute-start = (f32[20,1,1024]{2,1,0:T(1,128)S(1)}, f32[20,1,1024]{2,1,0:T(1,128)S(1)}, u32[]{:S(2)}, u32[]{:S(2)}) collective-permute-start(f32[20,1,1024]{2,1,0:T(1,128)S(1)} %get-tuple-element.23), channel_id=1, source_target_pairs={{0,16},{16,32},{32,48},{48,64},{64,80},{80,96},{96,112},{112,128},... | collective-permute-start | bytes 245768 | tf_op jit(solution)/shard_map/ppermute | solution.py:20
  13.4 14.0 %collective-permute-start.1 = (f32[20,1,1024]{2,1,0:T(1,128)S(1)}, f32[20,1,1024]{2,1,0:T(1,128)S(1)}, u32[]{:S(2)}, u32[]{:S(2)}) collective-permute-start(f32[20,1,1024]{2,1,0:T(1,128)S(1)} %get-tuple-element.24), channel_id=1, source_target_pairs={{16,0},{32,16},{48,32},{64,48},{80,64},{96,80},{112,96},{128,112},... | collective-permute-start | bytes 245768 | tf_op jit(solution)/shard_map/ppermute | solution.py:22
  29.6 1.7 copy-done.2
  32.8 4.0 %collective-permute-start.2 = (f32[20,34,1]{2,1,0:T(8,128)S(1)}, f32[20,34,1]{2,1,0:T(8,128)S(1)}, u32[]{:S(2)}, u32[]{:S(2)}) collective-permute-start(f32[20,34,1]{2,1,0:T(8,128)S(1)} %get-tuple-element.20), channel_id=1, source_target_pairs={{0,4},{4,8},{8,12},{1,5},{5,9},{9,13},{2,6},{6,10},{10,14},{3,7},{... | collective-permute-start | bytes 8168 | tf_op jit(solution)/shard_map/ppermute | solution.py:20
  37.5 2.6 %collective-permute-done.3 = f32[20,34,1]{2,1,0:T(8,128)S(1)} collective-permute-done((f32[20,34,1]{2,1,0:T(8,128)S(1)}, f32[20,34,1]{2,1,0:T(8,128)S(1)}, u32[]{:S(2)}, u32[]{:S(2)}) %collective-permute-start.3) | collective-permute-done | bytes 2752 | tf_op jit(solution)/shard_map/ppermute | solution.py:22
  41.6 4.9 %concatenate.46 = f32[20,34,1026]{2,1,0:T(8,128)} concatenate(f32[20,34,1]{2,1,0:T(8,128)S(1)} %collective-permute-done.2, f32[20,34,1024]{2,1,0:T(8,128)} %copy-done.2, f32[20,34,1]{2,1,0:T(8,128)S(1)} %collective-permute-done.3), dimensions={2} | concatenate | bytes 5581440 | tf_op jit(solution)/shard_map/concatenate | solution.py:18
  46.5 1.9 slice_bitcast_fusion.6
  49.0 3.2 %subtract_multiply_fusion.3 = f32[16,32,1025]{2,1,0:T(8,128)} fusion(f32[20,34,1]{2,1,0:T(8,128)S(1)} %collective-permute-done.3, f32[20,1,1024]{2,1,0:T(1,128)S(1)} %copy-done.8, f32[20,32,1024]{2,1,0:T(8,128)S(1)} %bitcast_dynamic-update-slice_fusion.1, f32[20,1,1024]{2,1,0:T(1,128)S(1)} %collective-permute-done, ...), kind=kLoop, calls=%fused_computation.21 | loop fusion | flops 6822400 | bytes 5283520 | tf_op jit(solution)/shard_map/mul | solution.py:50
  52.2 2.3 subtract_multiply_fusion.1
  54.5 51.6 %all-reduce.3.cloned.1.call-done = f32[32,1024]{1,0:T(8,128)} async-done(((f32[32,1024]{1,0:T(8,128)}), f32[32,1024]{1,0:T(8,128)}) %all-reduce.3.cloned.1.call-update) | async-done | bytes 131088 | tf_op jit(solution)/shard_map/psum | solution.py:62
  107.1 6.3 %fusion.14 = (f32[32,1024]{1,0:T(8,128)}, f32[16,32,1024]{2,1,0:T(8,128)S(1)}) fusion(f32[16,32,1024]{2,1,0:T(8,128)} %param.7, f32[32,1024]{1,0:T(8,128)S(1)} %slice_multiply_fusion.5, f32[16]{0:T(128)S(1)} %copy-done.17, f32[16,32,1025]{2,1,0:T(8,128)} %subtract_multiply_fusion.3, f32[16,33,1024]{2,1,0:T(8,128)} %subtract_multiply_fusion.1), kind=kLoop, calls=%fused_computation.82 | loop fusion | flops 5210112 | bytes 12845120 | tf_op jit(solution)/shard_map/reduce_sum | solution.py:82
  115.3 5.0 %collective-permute-start.5 = (f32[20,1,1024]{2,0,1:T(8,128)S(1)}, f32[20,1,1024]{2,0,1:T(8,128)S(1)}, u32[]{:S(2)}, u32[]{:S(2)}) collective-permute-start(f32[20,1,1024]{2,0,1:T(8,128)S(1)} %copy.26), channel_id=1, source_target_pairs={{16,0},{32,16},{48,32},{64,48},{80,64},{96,80},{112,96},{128,112},... | collective-permute-start | bytes 245768 | tf_op jit(solution)/shard_map/ppermute | solution.py:22
  120.4 1.9 collective-permute-start.4
  122.5 12.4 %collective-permute-done.4 = f32[20,1,1024]{2,0,1:T(8,128)S(1)} collective-permute-done((f32[20,1,1024]{2,0,1:T(8,128)S(1)}, f32[20,1,1024]{2,0,1:T(8,128)S(1)}, u32[]{:S(2)}, u32[]{:S(2)}) %collective-permute-start.4) | collective-permute-done | bytes 81952 | tf_op jit(solution)/shard_map/ppermute | solution.py:20
  138.4 3.1 %collective-permute-start.6 = (f32[20,34,1]{2,1,0:T(8,128)}, f32[20,34,1]{2,1,0:T(8,128)S(1)}, u32[]{:S(2)}, u32[]{:S(2)}) collective-permute-start(f32[20,34,1]{2,1,0:T(8,128)} %get-tuple-element.17), channel_id=1, source_target_pairs={{0,4},{4,8},{8,12},{1,5},{5,9},{9,13},{2,6},{6,10},{10,14},{3,7},{... | collective-permute-start | bytes 8168 | tf_op jit(solution)/shard_map/ppermute | solution.py:20
  143.0 6.2 %collective-permute-done.6 = f32[20,34,1]{2,1,0:T(8,128)S(1)} collective-permute-done((f32[20,34,1]{2,1,0:T(8,128)}, f32[20,34,1]{2,1,0:T(8,128)S(1)}, u32[]{:S(2)}, u32[]{:S(2)}) %collective-permute-start.6) | collective-permute-done | bytes 2752 | tf_op jit(solution)/shard_map/ppermute | solution.py:20
  149.2 3.8 %collective-permute-done.7 = f32[20,34,1]{2,1,0:T(8,128)S(1)} collective-permute-done((f32[20,34,1]{2,1,0:T(8,128)}, f32[20,34,1]{2,1,0:T(8,128)S(1)}, u32[]{:S(2)}, u32[]{:S(2)}) %collective-permute-start.7) | collective-permute-done | bytes 2752 | tf_op jit(solution)/shard_map/ppermute | solution.py:22
  153.0 4.9 %concatenate.53 = f32[20,34,1026]{2,1,0:T(8,128)} concatenate(f32[20,34,1]{2,1,0:T(8,128)S(1)} %collective-permute-done.6, f32[20,34,1024]{2,1,0:T(8,128)} %copy-done.1, f32[20,34,1]{2,1,0:T(8,128)S(1)} %collective-permute-done.7), dimensions={2} | concatenate | bytes 5581440 | tf_op jit(solution)/shard_map/concatenate | solution.py:18
  157.9 2.0 slice_bitcast_fusion
  160.4 3.2 %subtract_multiply_fusion.2 = f32[16,32,1025]{2,1,0:T(8,128)} fusion(f32[20,34,1]{2,1,0:T(8,128)S(1)} %collective-permute-done.7, f32[20,1,1024]{2,1,0:T(1,128)S(1)} %copy.28, f32[20,32,1024]{2,1,0:T(8,128)S(1)} %bitcast_dynamic-update-slice_fusion, f32[20,1,1024]{2,1,0:T(1,128)S(1)} %copy-done.4, f32[20,34,1]{2,1,0:T(8,128)S(1)} %collective-permute-done.6, ...), kind=kLoop, calls=%fused_computation.20 | loop fusion | flops 6822400 | bytes 5283520 | tf_op jit(solution)/shard_map/mul | solution.py:50
  163.6 2.3 subtract_multiply_fusion
  165.9 53.9 %all-reduce.5.cloned.1.call-done = f32[32,1024]{1,0:T(8,128)} async-done(((f32[32,1024]{1,0:T(8,128)}), f32[32,1024]{1,0:T(8,128)}) %all-reduce.5.cloned.1.call-update) | async-done | bytes 131088 | tf_op jit(solution)/shard_map/psum | solution.py:62
  220.8 8.0 %fusion.5 = f32[16,32,1024]{2,1,0:T(8,128)} fusion(f32[16,32,1024]{2,1,0:T(8,128)} %param.7, f32[16,32,1024]{2,1,0:T(8,128)} %copy-done, f32[16,32,1025]{2,1,0:T(8,128)} %subtract_multiply_fusion.2, f32[16,33,1024]{2,1,0:T(8,128)} %subtract_multiply_fusion, f32[32,1024]{1,0:T(8,128)S(1)} %slice_multiply_fusion.4, f32[16]{0:T(128)S(1)} %copy-done.18), kind=kLoop, calls=%fused_computation.28 | loop fusion | flops 5767168 | bytes 14811200 | tf_op jit(solution)/shard_map/add | solution.py:84
  (81 shorter events, 16.0 us)
Async XLA Ops:
  6.5 2.6 %copy-start.13 = (f32[32,1024]{1,0:T(8,128)S(1)}, f32[32,1024]{1,0:T(8,128)}, u32[]{:S(2)}) copy-start(f32[32,1024]{1,0:T(8,128)} %param.10) | copy-start | bytes 393220
  6.5 2.6 %copy-start.15 = (f32[32,1024]{1,0:T(8,128)S(1)}, f32[32,1024]{1,0:T(8,128)}, u32[]{:S(2)}) copy-start(f32[32,1024]{1,0:T(8,128)} %param.11) | copy-start | bytes 393220
  6.5 2.6 %copy-start.5 = (s32[32,1024]{1,0:T(8,128)S(1)}, s32[32,1024]{1,0:T(8,128)}, u32[]{:S(2)}) copy-start(s32[32,1024]{1,0:T(8,128)} %param.13) | copy-start | bytes 393220
  6.5 2.7 %copy-start.11 = (f32[32,1024]{1,0:T(8,128)S(1)}, f32[32,1024]{1,0:T(8,128)}, u32[]{:S(2)}) copy-start(f32[32,1024]{1,0:T(8,128)} %param.12) | copy-start | bytes 393220
  6.5 99.6 %all-reduce.3.cloned.1.call-start = ((), (), s32[]{:S(2)}) async-start(), calls=%async_computation | async-start | bytes 262144 | tf_op jit(solution)/shard_map/psum | solution.py:62
  9.4 18.2 %collective-permute-start = (f32[20,1,1024]{2,1,0:T(1,128)S(1)}, f32[20,1,1024]{2,1,0:T(1,128)S(1)}, u32[]{:S(2)}, u32[]{:S(2)}) collective-permute-start(f32[20,1,1024]{2,1,0:T(1,128)S(1)} %get-tuple-element.23), channel_id=1, source_target_pairs={{0,16},{16,32},{32,48},{48,64},{64,80},{80,96},{96,112},{112,128},... | collective-permute-start | bytes 245768 | tf_op jit(solution)/shard_map/ppermute | solution.py:20
  13.4 15.5 %collective-permute-start.1 = (f32[20,1,1024]{2,1,0:T(1,128)S(1)}, f32[20,1,1024]{2,1,0:T(1,128)S(1)}, u32[]{:S(2)}, u32[]{:S(2)}) collective-permute-start(f32[20,1,1024]{2,1,0:T(1,128)S(1)} %get-tuple-element.24), channel_id=1, source_target_pairs={{16,0},{32,16},{48,32},{64,48},{80,64},{96,80},{112,96},{128,112},... | collective-permute-start | bytes 245768 | tf_op jit(solution)/shard_map/ppermute | solution.py:22
  27.5 192.3 %all-reduce.5.cloned.1.call-start = ((), (), s32[]{:S(2)}) async-start(), calls=%async_computation.1 | async-start | bytes 262144 | tf_op jit(solution)/shard_map/psum | solution.py:62
  27.6 9.2 %copy-start.19 = (f32[64]{0:T(128)S(1)}, f32[64]{0:T(128)}, u32[]{:S(2)}) copy-start(f32[64]{0:T(128)} %param.9) | copy-start | bytes 772
  27.6 9.2 %copy-start.20 = (s32[16]{0:T(128)S(1)}, s32[16]{0:T(128)}, u32[]{:S(2)}) copy-start(s32[16]{0:T(128)} %param.8) | copy-start | bytes 196
  29.6 1.7 copy-start.2
  31.5 8.7 %collective-permute-start.3 = (f32[20,34,1]{2,1,0:T(8,128)S(1)}, f32[20,34,1]{2,1,0:T(8,128)S(1)}, u32[]{:S(2)}, u32[]{:S(2)}) collective-permute-start(f32[20,34,1]{2,1,0:T(8,128)S(1)} %get-tuple-element.19), channel_id=1, source_target_pairs={{4,0},{8,4},{12,8},{5,1},{9,5},{13,9},{6,2},{10,6},{14,10},{7,3},{... | collective-permute-start | bytes 8168 | tf_op jit(solution)/shard_map/ppermute | solution.py:22
  32.8 8.9 %collective-permute-start.2 = (f32[20,34,1]{2,1,0:T(8,128)S(1)}, f32[20,34,1]{2,1,0:T(8,128)S(1)}, u32[]{:S(2)}, u32[]{:S(2)}) collective-permute-start(f32[20,34,1]{2,1,0:T(8,128)S(1)} %get-tuple-element.20), channel_id=1, source_target_pairs={{0,4},{4,8},{8,12},{1,5},{5,9},{9,13},{2,6},{6,10},{10,14},{3,7},{... | collective-permute-start | bytes 8168 | tf_op jit(solution)/shard_map/ppermute | solution.py:20
  46.5 2.5 %copy-start.8 = (f32[20,1,1024]{2,1,0:T(1,128)S(1)}, f32[20,1,1024]{2,1,0:T(1,128)}, u32[]{:S(2)}) copy-start(f32[20,1,1024]{2,1,0:T(1,128)} %copy-done.7) | copy-start | bytes 245764
  52.2 53.9 %copy-start.9 = (f32[34,1026]{1,0:T(8,128)S(1)}, f32[34,1026]{1,0:T(8,128)}, u32[]{:S(2)}) copy-start(f32[34,1026]{1,0:T(8,128)} %get-tuple-element.14) | copy-start | bytes 418612
  52.2 54.9 %copy-start.17 = (f32[16]{0:T(128)S(1)}, f32[16]{0:T(128)}, u32[]{:S(2)}) copy-start(f32[16]{0:T(128)} %select_reduce_fusion) | copy-start | bytes 196
  115.3 7.1 %collective-permute-start.5 = (f32[20,1,1024]{2,0,1:T(8,128)S(1)}, f32[20,1,1024]{2,0,1:T(8,128)S(1)}, u32[]{:S(2)}, u32[]{:S(2)}) collective-permute-start(f32[20,1,1024]{2,0,1:T(8,128)S(1)} %copy.26), channel_id=1, source_target_pairs={{16,0},{32,16},{48,32},{64,48},{80,64},{96,80},{112,96},{128,112},... | collective-permute-start | bytes 245768 | tf_op jit(solution)/shard_map/ppermute | solution.py:22
  120.4 14.5 %collective-permute-start.4 = (f32[20,1,1024]{2,0,1:T(8,128)S(1)}, f32[20,1,1024]{2,0,1:T(8,128)S(1)}, u32[]{:S(2)}, u32[]{:S(2)}) collective-permute-start(f32[20,1,1024]{2,0,1:T(8,128)S(1)} %copy.25), channel_id=1, source_target_pairs={{0,16},{16,32},{32,48},{48,64},{64,80},{80,96},{96,112},{112,128},... | collective-permute-start | bytes 245768 | tf_op jit(solution)/shard_map/ppermute | solution.py:20
  135.6 1.7 copy-start.1
  138.4 10.9 %collective-permute-start.6 = (f32[20,34,1]{2,1,0:T(8,128)}, f32[20,34,1]{2,1,0:T(8,128)S(1)}, u32[]{:S(2)}, u32[]{:S(2)}) collective-permute-start(f32[20,34,1]{2,1,0:T(8,128)} %get-tuple-element.17), channel_id=1, source_target_pairs={{0,4},{4,8},{8,12},{1,5},{5,9},{9,13},{2,6},{6,10},{10,14},{3,7},{... | collective-permute-start | bytes 8168 | tf_op jit(solution)/shard_map/ppermute | solution.py:20
  141.5 11.5 %collective-permute-start.7 = (f32[20,34,1]{2,1,0:T(8,128)}, f32[20,34,1]{2,1,0:T(8,128)S(1)}, u32[]{:S(2)}, u32[]{:S(2)}) collective-permute-start(f32[20,34,1]{2,1,0:T(8,128)} %get-tuple-element.18), channel_id=1, source_target_pairs={{4,0},{8,4},{12,8},{5,1},{9,5},{13,9},{6,2},{10,6},{14,10},{7,3},{... | collective-permute-start | bytes 8168 | tf_op jit(solution)/shard_map/ppermute | solution.py:22
  157.9 2.5 %copy-start.4 = (f32[20,1,1024]{2,1,0:T(1,128)S(1)}, f32[20,1,1024]{2,1,0:T(1,128)}, u32[]{:S(2)}) copy-start(f32[20,1,1024]{2,1,0:T(1,128)} %copy-done.3) | copy-start | bytes 245764
  163.6 56.2 %copy-start.10 = (f32[34,1026]{1,0:T(8,128)S(1)}, f32[34,1026]{1,0:T(8,128)}, u32[]{:S(2)}) copy-start(f32[34,1026]{1,0:T(8,128)} %get-tuple-element.9) | copy-start | bytes 418612
  163.6 57.2 %copy-start.18 = (f32[16]{0:T(128)S(1)}, f32[16]{0:T(128)}, u32[]{:S(2)}) copy-start(f32[16]{0:T(128)} %select_reduce_fusion) | copy-start | bytes 196
  (7 other events, 8.0 us)
Sparse Core Ops, SparseCore 0:
  27.6 78.4 all-reduce.2
  143.1 76.6 all-reduce.4
where the time goes:
time: 236 us
  waiting for transfers between devices  133 us (56%)
  starting transfers between devices  35 us (15%)
  other arithmetic  32.7 us (14%)
  local copies, waits for them, and re-layouts  20.7 us (9%)
  between operations  13.8 us (6%)
    psum x2, waiting for transfers between devices, hindered(): solids = lax.psum(partial_solids, 'cls')  105 us
    ppermute x4, starting transfers between devices, padded(): lax.ppermute(head, axis, [((i + 1) % count, i) for i in range(ends)])  21.8 us
    ppermute x4, waiting for transfers between devices, padded(): lax.ppermute(tail, axis, [(i, (i + 1) % count) for i in range(ends)])  20.2 us
    ppermute x4, starting transfers between devices, padded(): lax.ppermute(tail, axis, [(i, (i + 1) % count) for i in range(ends)])  13.1 us
    mul x4, other arithmetic, tendency(): opening * (jnp.maximum(face_speed, 0.0) * lower_cells + jnp.minimum(face_...  11 us
    concatenate x2, local copies, waits for them, and re-layouts, padded(): jnp.concatenate([lax.ppermute(tail, axis, [(i, (i + 1) % count) for i in...  9.79 us
    add x1, other arithmetic, per_device(): return 0.5 * concentration + 0.5 * section_two  8.01 us
    ppermute x4, waiting for transfers between devices, padded(): lax.ppermute(head, axis, [((i + 1) % count, i) for i in range(ends)])  7.78 us
  transfers between devices with their start and end apart: 10, of which 9 were waited for; matrix products, arithmetic and copies ran while one was open for 12% of the time, Pallas kernels for 0%

commit v1 on v0

v1 whole, which is shorter than its diff:
```python
import jax
import jax.numpy as jnp
from jax import lax
from jax.experimental import pallas as pl
from jax.experimental.pallas import tpu as pltpu
from jax.sharding import PartitionSpec as P

TIME_STEP = 0.25
DIFFUSION = 0.1
VOLUME_PER_UNIT = 0.01
EXPONENT = 4.65

MESH = pl.DeviceIdType.MESH
SUB, LANE = 8, 128
ALONG, ACROSS, WETTED = 0, 1, 2


def hindered(solids):
    return jnp.exp(EXPONENT * jnp.log(1.0 - VOLUME_PER_UNIT * solids))


def section_kernel(
    conc,
    table,
    settle,
    along,
    across,
    depth,
    mask,
    out,
    field,
    first,
    total,
    partial,
    sibling,
    remote,
    bed,
    coef,
    gain,
    moved,
    depth_v,
    mask_v,
    pack,
    load_sem,
    out_sem,
    send_sem,
    recv_sem,
):
    classes, rows, cols = conc.shape
    row_tiles, col_tiles = rows // SUB, cols // LANE
    helix, cross, cls = lax.axis_index("helix"), lax.axis_index("cross"), lax.axis_index("cls")
    n_helix, n_cross = lax.axis_size("helix"), lax.axis_size("cross")
    core, half = cls % 2, cls // 2
    me_sibling = (helix, cross, half * 2 + 1 - core)
    me_partner = (helix, cross, (1 - half) * 2 + core)
    me_prev = ((helix + n_helix - 1) % n_helix, cross, cls)
    me_next = ((helix + 1) % n_helix, cross, cls)
    me_left = (helix, (cross + n_cross - 1) % n_cross, cls)
    me_right = (helix, (cross + 1) % n_cross, cls)

    inner_cols = pl.ds(LANE, cols)

    loads = []
    for r in range(row_tiles):
        loads.append(
            pltpu.make_async_copy(
                conc.at[:, pl.ds(r * SUB, SUB), :],
                field.at[pl.ds(0, classes), pl.ds(SUB + r * SUB, SUB), inner_cols],
                load_sem.at[r],
            )
        )
    statics = [
        pltpu.make_async_copy(
            along, field.at[classes + ALONG, pl.ds(SUB, rows), inner_cols], load_sem.at[row_tiles]
        ),
        pltpu.make_async_copy(
            across, field.at[classes + ACROSS, pl.ds(SUB, rows), inner_cols], load_sem.at[row_tiles + 1]
        ),
        pltpu.make_async_copy(depth, depth_v, load_sem.at[row_tiles + 2]),
        pltpu.make_async_copy(mask, mask_v, load_sem.at[row_tiles + 3]),
    ]
    for copy in loads + statics:
        copy.start()

    barrier = pltpu.get_barrier_semaphore()
    peers = (me_sibling, me_partner, me_prev, me_next, me_left, me_right)
    for peer in peers:
        pl.semaphore_signal(barrier, inc=1, device_id=peer, device_id_type=MESH)

    speed = [settle[table[k]] for k in range(classes)]
    sub = lax.broadcasted_iota(jnp.int32, (SUB, LANE), 0)
    lane = lax.broadcasted_iota(jnp.int32, (SUB, LANE), 1)

    def tile(ref, plane, r, j):
        return ref[
            plane,
            pl.ds(pl.multiple_of(SUB + r * SUB, SUB), SUB),
            pl.ds(pl.multiple_of(LANE + j * LANE, LANE), LANE),
        ]

    def put(ref, plane, r, j, value):
        ref[
            plane,
            pl.ds(pl.multiple_of(SUB + r * SUB, SUB), SUB),
            pl.ds(pl.multiple_of(LANE + j * LANE, LANE), LANE),
        ] = value

    def at(r, j):
        return pl.ds(pl.multiple_of(r * SUB, SUB), SUB), pl.ds(pl.multiple_of(j * LANE, LANE), LANE)

    def north(ref, plane, r, j, x):
        return pltpu.roll(jnp.where(sub == SUB - 1, tile(ref, plane, r - 1, j), x), 1, 0)

    def south(ref, plane, r, j, x):
        return pltpu.roll(jnp.where(sub == 0, tile(ref, plane, r + 1, j), x), SUB - 1, 0)

    def west(ref, plane, r, j, x):
        return pltpu.roll(jnp.where(lane == LANE - 1, tile(ref, plane, r, j - 1), x), 1, 1)

    def east(ref, plane, r, j, x):
        return pltpu.roll(jnp.where(lane == 0, tile(ref, plane, r, j + 1), x), LANE - 1, 1)

    def over_cols(body):
        def step(j, carry):
            body(j)
            return carry

        lax.fori_loop(0, col_tiles, step, 0)

    def over_tiles(body, tiles):
        def step(i, carry):
            body(tiles[0] + i // col_tiles * tiles[1], i % col_tiles)
            return carry

        lax.fori_loop(0, tiles[2] * col_tiles, step, 0)

    for r in range(row_tiles):
        loads[r].wait()

        def sums(j):
            parts_s, parts_w = [], []
            for k in range(classes):
                x = tile(field, k, r, j)
                parts_s.append(x)
                parts_w.append(speed[k] * x)
            while len(parts_s) > 1:
                parts_s = [a + b for a, b in zip(parts_s[::2], parts_s[1::2])]
                parts_w = [a + b for a, b in zip(parts_w[::2], parts_w[1::2])]
            partial[(0, *at(r, j))] = parts_s[0]
            partial[(1, *at(r, j))] = parts_w[0]

        over_cols(sums)

    for copy in statics:
        copy.wait()

    def statics_of(r, j):
        kind = mask_v[at(r, j)]
        put(field, classes + WETTED, r, j, (kind > 0).astype(jnp.float32))
        bed[at(r, j)] = jnp.where(kind == 2, TIME_STEP, 0.0) / depth_v[at(r, j)]

    over_tiles(statics_of, (0, 1, row_tiles))

    def pack_cols(ref, planes, slot):
        for r in range(row_tiles):
            head = jnp.zeros((SUB, LANE), jnp.float32)
            tail = jnp.zeros((SUB, LANE), jnp.float32)
            for p in range(planes):
                x = tile(ref, p, r, 0)
                head = jnp.where(lane == p, pltpu.roll(x, p, 1) if p else x, head)
                x = tile(ref, p, r, col_tiles - 1)
                tail = jnp.where(lane == p, pltpu.roll(x, p + 1, 1), tail)
            pack[(slot, *at(r, 0))] = head
            pack[(slot + 1, *at(r, 0))] = tail

    def unpack_cols(ref, planes, slot, walls):
        for r in range(row_tiles):
            head = pack[(slot + 2, *at(r, 0))]
            tail = pack[(slot + 3, *at(r, 0))]
            for p in range(planes):
                right = pltpu.roll(head, LANE - p, 1) if p else head
                left = pltpu.roll(tail, LANE - 1 - p, 1)
                if p in walls:
                    right = jnp.where(cross < n_cross - 1, right, 0.0)
                    left = jnp.where(cross > 0, left, 0.0)
                put(ref, p, r, col_tiles, right)
                put(ref, p, r, -1, left)

    pack_cols(field, classes + 3, 0)

    def send(index, src, dst, peer):
        copy = pltpu.make_async_remote_copy(
            src_ref=src,
            dst_ref=dst,
            send_sem=send_sem.at[index],
            recv_sem=recv_sem.at[index],
            device_id=peer,
            device_id_type=MESH,
        )
        copy.start()
        return copy

    pl.semaphore_wait(barrier, len(peers))

    shares = [send(q, partial.at[q], sibling.at[q], me_sibling) for q in range(2)]

    def send_halos(index, ref, planes, slot):
        every = pl.ds(0, planes)
        return [
            send(index, ref.at[every, pl.ds(SUB + rows - 1, 1), inner_cols], ref.at[every, pl.ds(SUB - 1, 1), inner_cols], me_next),
            send(index + 1, ref.at[every, pl.ds(SUB, 1), inner_cols], ref.at[every, pl.ds(SUB + rows, 1), inner_cols], me_prev),
        ]

    def send_cols(index, slot):
        return [
            send(index, pack.at[slot], pack.at[slot + 2], me_left),
            send(index + 1, pack.at[slot + 1], pack.at[slot + 3], me_right),
        ]

    def own_rows(t):
        return pl.ds(pl.multiple_of(SUB * (t + core * (row_tiles - 1 - 2 * t)), SUB), SUB)

    def other_rows(t):
        return pl.ds(pl.multiple_of(SUB * (t + (1 - core) * (row_tiles - 1 - 2 * t)), SUB), SUB)

    steps = row_tiles // 2
    far = []
    for q in range(2):
        shares[q].wait()
        for t in range(steps):
            own = own_rows(t)
            partial_sum = partial[q, own, :] + sibling[q, own, :]
            total[q, own, :] = partial_sum
            far.append(send(2 + q * steps + t, total.at[q, own, :], remote.at[q, own, :], me_partner))
        for t in range(steps):
            other = other_rows(t)
            total[q, other, :] = partial[q, other, :] + sibling[q, other, :]
    base = 2 + 2 * steps
    row_halo = send_halos(base, field, classes + 3, 0)
    col_halo = send_cols(base + 2, 0)

    for copy in col_halo + row_halo:
        copy.wait_recv()
    unpack_cols(field, classes + 3, 0, (classes + WETTED,))

    def coefficients(r, j):
        u = tile(field, classes + ALONG, r, j)
        v = tile(field, classes + ACROSS, r, j)
        w = tile(field, classes + WETTED, r, j)

        def face(speed_a, speed_b, wet_b):
            face_speed = 0.5 * (speed_a + speed_b)
            opening = TIME_STEP * (w * wet_b)
            ahead = opening * (jnp.maximum(face_speed, 0.0) + DIFFUSION)
            back = opening * (DIFFUSION - jnp.minimum(face_speed, 0.0))
            return ahead, back

        wet = classes + WETTED
        from_north, to_north = face(u, north(field, classes + ALONG, r, j, u), north(field, wet, r, j, w))
        to_south, from_south = face(u, south(field, classes + ALONG, r, j, u), south(field, wet, r, j, w))
        from_west, to_west = face(v, west(field, classes + ACROSS, r, j, v), west(field, wet, r, j, w))
        to_east, from_east = face(v, east(field, classes + ACROSS, r, j, v), east(field, wet, r, j, w))
        coef[(0, *at(r, j))] = from_north
        coef[(1, *at(r, j))] = from_south
        coef[(2, *at(r, j))] = from_west
        coef[(3, *at(r, j))] = from_east
        coef[(4, *at(r, j))] = 1.0 - ((to_north + to_south) + (to_west + to_east))

    over_tiles(coefficients, (0, 1, row_tiles))

    def transported(ref, plane, r, j, factors):
        x = tile(ref, plane, r, j)
        along_part = factors[0] * north(ref, plane, r, j, x) + factors[1] * south(ref, plane, r, j, x)
        across_part = factors[2] * west(ref, plane, r, j, x) + factors[3] * east(ref, plane, r, j, x)
        return factors[4] * x + (along_part + across_part)

    def carry_first(r, j):
        factors = [coef[(i, *at(r, j))] for i in range(5)]
        for k in range(classes):
            put(first, k, r, j, transported(field, k, r, j, factors))

    over_tiles(carry_first, (0, 1, row_tiles))

    def receive(q, t):
        far[q * steps + t].wait_recv()
        own = own_rows(t)
        return send(base + 8 + q * steps + t, remote.at[q, own, :], remote.at[q, own, :], me_sibling)

    def arrived(q, t):
        pltpu.make_async_remote_copy(
            src_ref=remote.at[q, other_rows(t), :],
            dst_ref=remote.at[q, other_rows(t), :],
            send_sem=send_sem.at[base + 8 + q * steps + t],
            recv_sem=recv_sem.at[base + 8 + q * steps + t],
            device_id=me_sibling,
            device_id_type=MESH,
        ).wait_recv()

    forwards = []

    def section_one(r, j):
        solids = total[(0, *at(r, j))] + remote[(0, *at(r, j))]
        put(first, classes, r, j, solids)
        g = bed[at(r, j)] * hindered(solids)
        gain[at(r, j)] = g
        for k in range(classes):
            put(first, k, r, j, tile(first, k, r, j) - (speed[k] * g) * tile(field, k, r, j))

    halos = None
    for t in range(steps):
        forwards.append(receive(0, t))
        arrived(0, t)
        over_tiles(section_one, (t, row_tiles - 1 - 2 * t, 2))
        if t == 0:
            row_halo_one = send_halos(base + 4, first, classes + 1, 4)
    pack_cols(first, classes + 1, 4)
    col_halo_one = send_cols(base + 6, 4)

    def carry_second(r, j):
        factors = [coef[(i, *at(r, j))] for i in range(5)]
        for k in range(classes):
            value = tile(field, k, r, j) + transported(first, k, r, j, factors)
            moved[(k, *at(r, j))] = 0.5 * value
        moved[(classes, *at(r, j))] = transported(first, classes, r, j, factors)

    for copy in col_halo_one:
        copy.wait_recv()
    unpack_cols(first, classes + 1, 4, ())
    over_tiles(carry_second, (1, 1, row_tiles - 2))
    for copy in row_halo_one:
        copy.wait_recv()
    over_tiles(carry_second, (0, row_tiles - 1, 2))

    def finish(r, j):
        weighted = total[(1, *at(r, j))] + remote[(1, *at(r, j))]
        solids = moved[(classes, *at(r, j))] - gain[at(r, j)] * weighted
        g = (0.5 * bed[at(r, j)]) * hindered(solids)
        for k in range(classes):
            moved[(k, *at(r, j))] = moved[(k, *at(r, j))] - (speed[k] * g) * tile(first, k, r, j)

    stores = []
    for t in range(steps):
        forwards.append(receive(1, t))
        arrived(1, t)
        over_tiles(finish, (t, row_tiles - 1 - 2 * t, 2))
        for r in (t, row_tiles - 1 - t):
            copy = pltpu.make_async_copy(
                moved.at[pl.ds(0, classes), pl.ds(r * SUB, SUB), :],
                out.at[:, pl.ds(r * SUB, SUB), :],
                out_sem.at[r],
            )
            copy.start()
            stores.append(copy)

    for copy in shares:
        pass
    for copy in far + row_halo + col_halo + forwards + row_halo_one + col_halo_one:
        copy.wait_send()
    for copy in stores:
        copy.wait()


def per_device(concentration, class_table, settle_speed, along_speed, across_speed, film_depth, cell_mask):
    classes, rows, cols = concentration.shape
    padded = (rows + 2 * SUB, cols + 2 * LANE)
    flat = (rows, cols)
    row_tiles = rows // SUB
    copies = 2 + 4 * (row_tiles // 2) + 8
    anywhere = pl.BlockSpec(memory_space=pl.ANY)
    scalars = pl.BlockSpec(memory_space=pltpu.SMEM)
    f32 = jnp.float32
    return pl.pallas_call(
        section_kernel,
        out_shape=jax.ShapeDtypeStruct(concentration.shape, f32),
        in_specs=[anywhere, scalars, scalars, anywhere, anywhere, anywhere, anywhere],
        out_specs=anywhere,
        scratch_shapes=[
            pltpu.VMEM((classes + 3, *padded), f32),
            pltpu.VMEM((classes + 1, *padded), f32),
            pltpu.VMEM((2, *flat), f32),
            pltpu.VMEM((2, *flat), f32),
            pltpu.VMEM((2, *flat), f32),
            pltpu.VMEM((2, *flat), f32),
            pltpu.VMEM(flat, f32),
            pltpu.VMEM((5, *flat), f32),
            pltpu.VMEM(flat, f32),
            pltpu.VMEM((classes + 1, *flat), f32),
            pltpu.VMEM(flat, f32),
            pltpu.VMEM(flat, jnp.int32),
            pltpu.VMEM((8, rows, LANE), f32),
            pltpu.SemaphoreType.DMA((row_tiles + 4,)),
            pltpu.SemaphoreType.DMA((row_tiles,)),
            pltpu.SemaphoreType.DMA((copies,)),
            pltpu.SemaphoreType.DMA((copies,)),
        ],
        compiler_params=pltpu.CompilerParams(
            collective_id=0, has_side_effects=True, vmem_limit_bytes=32 * 2**20
        ),
        cost_estimate=pl.CostEstimate(
            flops=40 * classes * rows * cols, bytes_accessed=8 * classes * rows * cols, transcendentals=4 * rows * cols
        ),
    )(concentration, class_table, settle_speed, along_speed, across_speed, film_depth, cell_mask)


def solution(mesh):
    grid = P("helix", "cross")
    return jax.shard_map(
        per_device,
        mesh=mesh,
        in_specs=(P("cls", "helix", "cross"), P("cls"), P(), grid, grid, grid, grid),
        out_specs=P("cls", "helix", "cross"),
        check_vma=False,
    )
```

time: 236 us -> 66.2 us (0.28)
  waiting for transfers between devices: 133 us -> 0 us
  Pallas kernels: 0 us -> 58.1 us
  starting transfers between devices: 35 us -> 0 us
  other arithmetic: 32.7 us -> 0 us
  between operations: 13.8 us -> 0.02 us
  local copies, waits for them, and re-layouts: 20.7 us -> 7.84 us
    psum x2 -> x0, waiting for transfers between devices: 105 us -> none  [hindered(): solids = lax.psum(partial_solids, 'cls')]
    pallas_call x0 -> x1, Pallas kernels: none -> 58.1 us  [per_device(): pl.pallas_call(section_kernel, out_shape=jax.ShapeDtypeStruct(concentrati...]
    ppermute x8 -> x0, starting transfers between devices: 34.9 us -> none  [the longest x4 21.8 us: padded(): lax.ppermute(head, axis, [((i + 1) % count, i) for i in range(ends)])]
    ppermute x8 -> x0, waiting for transfers between devices: 27.9 us -> none  [the longest x4 20.2 us: padded(): lax.ppermute(tail, axis, [(i, (i + 1) % count) for i in range(ends)])]
    mul x10 -> x0, other arithmetic: 13.5 us -> none  [the longest x4 11 us: tendency(): opening * (jnp.maximum(face_speed, 0.0) * lower_cells + jnp.minimum(face_...]
    concatenate x2 -> x0, local copies, waits for them, and re-layouts: 9.79 us -> none  [padded(): jnp.concatenate([lax.ppermute(tail, axis, [(i, (i + 1) % count) for i in...]
    reduce_sum x3 -> x0, other arithmetic: 9.62 us -> none  [the longest x1 6.32 us: per_device(): hindrance = hindered(jnp.sum(section_one, axis=0))]
    add x1 -> x0, other arithmetic: 8.01 us -> none  [per_device(): return 0.5 * concentration + 0.5 * section_two]
  transfers between devices with their start and end apart: 10 -> 0, of which waited for: 9 -> 0; matrix products, arithmetic and copies ran while one was open for 12% -> 0% of each run, Pallas kernels for 0% -> 0%
where the time goes in v1:
time: 66.2 us; the launch traced here: 66 us
  Pallas kernels  58.1 us (88%)
  local copies, waits for them, and re-layouts  7.84 us (12%)
    pallas_call x1, Pallas kernels, per_device(): pl.pallas_call(section_kernel, out_shape=jax.ShapeDtypeStruct(concentrati...  58.1 us
    unnamed x15, local copies, waits for them, and re-layouts  7.84 us

profile of v1, /device:TPU:1, one launch (start us, length us, event | category | flops | bytes accessed | tf_op | source)
XLA Modules:
  0.0 66.0 jit_solution(15728985171082116081)
XLA Ops:
  0.0 0.0 copy-start
  0.0 1.6 %copy-done = f32[16,32,1024]{2,1,0:T(8,128)S(1)} copy-done((f32[16,32,1024]{2,1,0:T(8,128)S(1)}, f32[16,32,1024]{2,1,0:T(8,128)}, u32[]{:S(2)}) %copy-start) | copy-done | bytes 2097176
  1.6 0.0 copy-start.1
  1.6 0.9 %copy-done.1 = f32[32,1024]{1,0:T(8,128)S(1)} copy-done((f32[32,1024]{1,0:T(8,128)S(1)}, f32[32,1024]{1,0:T(8,128)}, u32[]{:S(2)}) %copy-start.1) | copy-done | bytes 131096
  2.5 0.0 copy-start.2
  2.5 0.9 %copy-done.2 = f32[32,1024]{1,0:T(8,128)S(1)} copy-done((f32[32,1024]{1,0:T(8,128)S(1)}, f32[32,1024]{1,0:T(8,128)}, u32[]{:S(2)}) %copy-start.2) | copy-done | bytes 131096
  3.4 0.0 copy-start.3
  3.4 0.9 %copy-done.3 = f32[32,1024]{1,0:T(8,128)S(1)} copy-done((f32[32,1024]{1,0:T(8,128)S(1)}, f32[32,1024]{1,0:T(8,128)}, u32[]{:S(2)}) %copy-start.3) | copy-done | bytes 131096
  4.3 0.0 copy-start.4
  4.3 0.9 %copy-done.4 = s32[32,1024]{1,0:T(8,128)S(1)} copy-done((s32[32,1024]{1,0:T(8,128)S(1)}, s32[32,1024]{1,0:T(8,128)}, u32[]{:S(2)}) %copy-start.4) | copy-done | bytes 131096
  5.2 0.0 copy-start.5
  5.2 0.7 copy-done.5
  5.9 0.0 copy-start.6
  5.9 0.7 copy-done.6
  6.5 58.1 %shard_map.73 = f32[16,32,1024]{2,1,0:T(8,128)S(1)} custom-call(f32[16,32,1024]{2,1,0:T(8,128)S(1)} %copy-done, s32[16]{0:T(128)S(1)} %copy-done.5, f32[64]{0:T(128)S(1)} %copy-done.6, f32[32,1024]{1,0:T(8,128)S(1)} %copy-done.1, f32[32,1024]{1,0:T(8,128)S(1)} %copy-done.2, f32[32,1024]{1,0:T(8,128)S(1)} %copy-done.3, s32[32,1024]{1,0:T(8,128)S(1)} %copy-done.4), custom_call_target="tpu_custom_call" | custom-call | flops 20971520 | bytes 4194304 | tf_op jit(solution)/shard_map/pallas_call | solution.py:372
  64.7 1.3 %copy.9 = f32[16,32,1024]{2,1,0:T(8,128)} copy(f32[16,32,1024]{2,1,0:T(8,128)S(1)} %shard_map.73) | data formatting | bytes 4194304
Async XLA Ops:
  0.0 1.6 %copy-start = (f32[16,32,1024]{2,1,0:T(8,128)S(1)}, f32[16,32,1024]{2,1,0:T(8,128)}, u32[]{:S(2)}) copy-start(f32[16,32,1024]{2,1,0:T(8,128)} %conc.1) | copy-start | bytes 6291460
  1.6 0.9 %copy-start.1 = (f32[32,1024]{1,0:T(8,128)S(1)}, f32[32,1024]{1,0:T(8,128)}, u32[]{:S(2)}) copy-start(f32[32,1024]{1,0:T(8,128)} %along.1) | copy-start | bytes 393220
  2.5 0.9 %copy-start.2 = (f32[32,1024]{1,0:T(8,128)S(1)}, f32[32,1024]{1,0:T(8,128)}, u32[]{:S(2)}) copy-start(f32[32,1024]{1,0:T(8,128)} %across.1) | copy-start | bytes 393220
  3.4 0.9 %copy-start.3 = (f32[32,1024]{1,0:T(8,128)S(1)}, f32[32,1024]{1,0:T(8,128)}, u32[]{:S(2)}) copy-start(f32[32,1024]{1,0:T(8,128)} %depth.1) | copy-start | bytes 393220
  4.3 0.9 %copy-start.4 = (s32[32,1024]{1,0:T(8,128)S(1)}, s32[32,1024]{1,0:T(8,128)}, u32[]{:S(2)}) copy-start(s32[32,1024]{1,0:T(8,128)} %mask.1) | copy-start | bytes 393220
  5.2 0.7 copy-start.5
  5.9 0.7 copy-start.6

commit v2 on v1

v2 whole, which is shorter than its diff:
```python
import jax
import jax.numpy as jnp
from jax import lax
from jax.experimental import pallas as pl
from jax.experimental.pallas import tpu as pltpu
from jax.sharding import PartitionSpec as P

TIME_STEP = 0.25
DIFFUSION = 0.1
VOLUME_PER_UNIT = 0.01
EXPONENT = 4.65

MESH = pl.DeviceIdType.MESH
SUB, LANE = 8, 128
ALONG, ACROSS, WETTED, BED = 0, 1, 2, 3


def hindered(solids):
    return jnp.exp(EXPONENT * jnp.log(1.0 - VOLUME_PER_UNIT * solids))


def section_kernel(
    conc,
    table,
    settle,
    along,
    across,
    depth,
    mask,
    out,
    table_s,
    settle_s,
    field,
    first,
    edges,
    total,
    partial,
    sibling,
    remote,
    coef,
    gain,
    moved,
    depth_v,
    mask_v,
    pack,
    corner,
    load_sem,
    send_sem,
    recv_sem,
):
    classes, rows, cols = conc.shape
    row_tiles, col_tiles = rows // SUB, cols // LANE
    helix, cross, cls = lax.axis_index("helix"), lax.axis_index("cross"), lax.axis_index("cls")
    n_helix, n_cross = lax.axis_size("helix"), lax.axis_size("cross")
    core, half = cls % 2, cls // 2
    me_sibling = (helix, cross, half * 2 + 1 - core)
    me_partner = (helix, cross, (1 - half) * 2 + core)
    me_prev = ((helix + n_helix - 1) % n_helix, cross, cls)
    me_next = ((helix + 1) % n_helix, cross, cls)
    far_prev = ((helix + n_helix - 1) % n_helix, cross, (1 - half) * 2 + core)
    far_next = ((helix + 1) % n_helix, cross, (1 - half) * 2 + core)
    me_left = (helix, (cross + n_cross - 1) % n_cross, cls)
    me_right = (helix, (cross + 1) % n_cross, cls)

    inner_cols = pl.ds(LANE, cols)
    last = row_tiles - 1
    steps = row_tiles // 2
    planes = classes + 4

    loads = [
        pltpu.make_async_copy(
            conc.at[:, pl.ds(r * SUB, SUB), :],
            field.at[pl.ds(0, classes), pl.ds(SUB + r * SUB, SUB), inner_cols],
            load_sem.at[r],
        )
        for r in range(row_tiles)
    ]
    scalars = [
        pltpu.make_async_copy(table, table_s, load_sem.at[row_tiles + 4]),
        pltpu.make_async_copy(settle, settle_s, load_sem.at[row_tiles + 5]),
    ]
    inner = pl.ds(SUB, rows)
    statics = [
        pltpu.make_async_copy(along, field.at[classes + ALONG, inner, inner_cols], load_sem.at[row_tiles]),
        pltpu.make_async_copy(across, field.at[classes + ACROSS, inner, inner_cols], load_sem.at[row_tiles + 1]),
        pltpu.make_async_copy(depth, depth_v, load_sem.at[row_tiles + 2]),
        pltpu.make_async_copy(mask, mask_v, load_sem.at[row_tiles + 3]),
    ]
    for copy in scalars + loads + statics:
        copy.start()

    barrier = pltpu.get_barrier_semaphore()
    peers = (me_sibling, me_partner, me_prev, me_next, far_prev, far_next, me_left, me_right)
    for peer in peers:
        pl.semaphore_signal(barrier, inc=1, device_id=peer, device_id_type=MESH)

    for copy in scalars:
        copy.wait()
    speed = [settle_s[table_s[k]] for k in range(classes)]
    sub = lax.broadcasted_iota(jnp.int32, (SUB, LANE), 0)
    lane = lax.broadcasted_iota(jnp.int32, (SUB, LANE), 1)

    def at(r, j):
        return pl.ds(pl.multiple_of(r * SUB, SUB), SUB), pl.ds(pl.multiple_of(j * LANE, LANE), LANE)

    def tile(ref, plane, r, j):
        return ref[(plane, *at(r + 1, j + 1))]

    def put(ref, plane, r, j, value):
        ref[(plane, *at(r + 1, j + 1))] = value

    def north(ref, plane, r, j, x, side=0):
        if side >= 0:
            x = jnp.where(sub == SUB - 1, tile(ref, plane, r - 1, j), x)
        return pltpu.roll(x, 1, 0)

    def south(ref, plane, r, j, x, side=0):
        if side <= 0:
            x = jnp.where(sub == 0, tile(ref, plane, r + 1, j), x)
        return pltpu.roll(x, SUB - 1, 0)

    def west(ref, plane, r, j, x):
        return pltpu.roll(jnp.where(lane == LANE - 1, tile(ref, plane, r, j - 1), x), 1, 1)

    def east(ref, plane, r, j, x):
        return pltpu.roll(jnp.where(lane == 0, tile(ref, plane, r, j + 1), x), LANE - 1, 1)

    def over(body, r0, rstep, nr, j0=0, jstep=1, nj=col_tiles, unroll=4):
        def step(i, carry):
            body(r0 + i // nj * rstep, j0 + i % nj * jstep)
            return carry

        lax.fori_loop(0, nr * nj, step, 0, unroll=unroll)

    def sums(r, j):
        parts_s, parts_w = [], []
        for k in range(classes):
            x = tile(field, k, r, j)
            parts_s.append(x)
            parts_w.append(speed[k] * x)
        while len(parts_s) > 1:
            parts_s = [a + b for a, b in zip(parts_s[::2], parts_s[1::2])]
            parts_w = [a + b for a, b in zip(parts_w[::2], parts_w[1::2])]
        partial[(0, *at(r, j))] = parts_s[0]
        partial[(1, *at(r, j))] = parts_w[0]

    for r in range(row_tiles):
        loads[r].wait()
        over(sums, r, 1, 1, unroll=2)

    used = []

    def send(src, dst, peer):
        index = len(used)
        used.append(index)
        copy = pltpu.make_async_remote_copy(
            src_ref=src,
            dst_ref=dst,
            send_sem=send_sem.at[index],
            recv_sem=recv_sem.at[index],
            device_id=peer,
            device_id_type=MESH,
        )
        copy.start()
        return copy

    pl.semaphore_wait(barrier, len(peers))

    shares = [send(partial.at[0], sibling.at[0], me_sibling)]

    def send_rows(start, count):
        some = pl.ds(start, count)
        return [
            send(
                field.at[some, pl.ds(SUB + rows - 2, 2), inner_cols],
                field.at[some, pl.ds(SUB - 2, 2), inner_cols],
                me_next,
            ),
            send(
                field.at[some, pl.ds(SUB, 2), inner_cols],
                field.at[some, pl.ds(SUB + rows, 2), inner_cols],
                me_prev,
            ),
        ]

    row_halo = send_rows(0, classes)
    shares.append(send(partial.at[1], sibling.at[1], me_sibling))

    for copy in statics:
        copy.wait()

    def statics_of(r, j):
        kind = mask_v[at(r, j)]
        put(field, classes + WETTED, r, j, (kind > 0).astype(jnp.float32))
        put(field, classes + BED, r, j, jnp.where(kind == 2, TIME_STEP, 0.0) / depth_v[at(r, j)])

    def own_rows(t):
        return pl.ds(pl.multiple_of(SUB * (t + core * (last - 2 * t)), SUB), SUB)

    def other_rows(t):
        return pl.ds(pl.multiple_of(SUB * (t + (1 - core) * (last - 2 * t)), SUB), SUB)

    far = []

    def chip_sums(q):
        shares[q].wait()
        for t in range(steps):
            own = own_rows(t)
            total[q, own, :] = partial[q, own, :] + sibling[q, own, :]
            far.append(send(total.at[q, own, :], remote.at[q, own, :], me_partner))
        for t in range(steps):
            other = other_rows(t)
            total[q, other, :] = partial[q, other, :] + sibling[q, other, :]

    chip_sums(0)
    edge_sums = []
    for source, after, before in ((0, me_next, me_prev), (1, far_next, far_prev)):
        edge_sums.append(
            send(total.at[0, pl.ds(rows - 1, 1), :], edges.at[source, 0, pl.ds(SUB - 1, 1), :], after)
        )
        edge_sums.append(send(total.at[0, pl.ds(0, 1), :], edges.at[source, 1, pl.ds(0, 1), :], before))

    over(statics_of, 0, 1, row_tiles)
    row_halo += send_rows(classes, 4)

    def pack_cols(ref, count, dst, slot, tile_rows):
        for i, r in enumerate(tile_rows):
            head = jnp.zeros((SUB, LANE), jnp.float32)
            tail = jnp.zeros((SUB, LANE), jnp.float32)
            for p in range(count):
                x = tile(ref, p, r, 0)
                head = jnp.where(lane == p, pltpu.roll(x, p, 1) if p else x, head)
                x = tile(ref, p, r, col_tiles - 1)
                tail = jnp.where(lane == p, pltpu.roll(x, p + 1, 1), tail)
            dst[(slot, *at(i, 0))] = head
            dst[(slot + 1, *at(i, 0))] = tail

    def send_cols(src, slot):
        return [
            send(src.at[slot], src.at[slot + 2], me_left),
            send(src.at[slot + 1], src.at[slot + 3], me_right),
        ]

    def unpack_cols(ref, count, src, slot, tile_rows, walls):
        for i, r in enumerate(tile_rows):
            head = src[(slot + 2, *at(i, 0))]
            tail = src[(slot + 3, *at(i, 0))]
            for p in range(count):
                right = pltpu.roll(head, LANE - p, 1) if p else head
                left = pltpu.roll(tail, LANE - 1 - p, 1)
                if p in walls:
                    right = jnp.where(cross < n_cross - 1, right, 0.0)
                    left = jnp.where(cross > 0, left, 0.0)
                put(ref, p, r, col_tiles, right)
                put(ref, p, r, -1, left)

    own_tiles = tuple(range(row_tiles))
    outer_tiles = (-1, row_tiles)
    walls = (classes + WETTED,)

    pack_cols(field, classes + 3, pack, 0, own_tiles)
    col_halo = send_cols(pack, 0)
    chip_sums(1)

    def coefficients(r, j, side=0):
        u = tile(field, classes + ALONG, r, j)
        v = tile(field, classes + ACROSS, r, j)
        w = tile(field, classes + WETTED, r, j)

        def face(speed_a, speed_b, wet_b):
            face_speed = 0.5 * (speed_a + speed_b)
            opening = TIME_STEP * (w * wet_b)
            ahead = opening * (jnp.maximum(face_speed, 0.0) + DIFFUSION)
            back = opening * (DIFFUSION - jnp.minimum(face_speed, 0.0))
            return ahead, back

        wet = classes + WETTED
        speed_plane = classes + ALONG
        from_north, to_north = face(
            u, north(field, speed_plane, r, j, u, side), north(field, wet, r, j, w, side)
        )
        to_south, from_south = face(
            u, south(field, speed_plane, r, j, u, side), south(field, wet, r, j, w, side)
        )
        from_west, to_west = face(v, west(field, classes + ACROSS, r, j, v), west(field, wet, r, j, w))
        to_east, from_east = face(v, east(field, classes + ACROSS, r, j, v), east(field, wet, r, j, w))
        coef[(0, *at(r + 1, j))] = from_north
        coef[(1, *at(r + 1, j))] = from_south
        coef[(2, *at(r + 1, j))] = from_west
        coef[(3, *at(r + 1, j))] = from_east
        coef[(4, *at(r + 1, j))] = 1.0 - ((to_north + to_south) + (to_west + to_east))

    def transported(ref, plane, r, j, factors, side=0):
        x = tile(ref, plane, r, j)
        along_part = factors[0] * north(ref, plane, r, j, x, side) + factors[1] * south(ref, plane, r, j, x, side)
        across_part = factors[2] * west(ref, plane, r, j, x) + factors[3] * east(ref, plane, r, j, x)
        return factors[4] * x + (along_part + across_part)

    def carry_first(r, j, side=0):
        factors = [coef[(i, *at(r + 1, j))] for i in range(5)]
        for k in range(classes):
            put(first, k, r, j, transported(field, k, r, j, factors, side))

    for copy in col_halo:
        copy.wait_recv()
    unpack_cols(field, classes + 3, pack, 0, own_tiles, walls)
    over(coefficients, 1, 1, row_tiles - 2)
    over(carry_first, 1, 1, row_tiles - 2)

    for copy in row_halo:
        copy.wait_recv()
    pack_cols(field, classes + 3, corner, 0, outer_tiles)
    corners = send_cols(corner, 0)
    over(coefficients, 0, last, 2)
    over(carry_first, 0, last, 2)
    for copy in corners:
        copy.wait_recv()
    unpack_cols(field, classes + 3, corner, 0, outer_tiles, walls)

    def section_one(r, j, solids, keep_gain):
        put(first, classes, r, j, solids)
        g = tile(field, classes + BED, r, j) * hindered(solids)
        if keep_gain:
            gain[at(r, j)] = g
        for k in range(classes):
            put(first, k, r, j, tile(first, k, r, j) - (speed[k] * g) * tile(field, k, r, j))

    for copy in edge_sums:
        copy.wait_recv()
    for side, r in ((-1, -1), (1, row_tiles)):

        def outer(_, j, side=side, r=r):
            coefficients(r, j, side)
            carry_first(r, j, side)
            low = 0 if side < 0 else 1
            strip = pl.ds(pl.multiple_of(j * LANE, LANE), LANE)
            section_one(r, j, edges[0, low, :, strip] + edges[1, low, :, strip], False)

        over(outer, r, 1, 1, unroll=2)

    forwards = []

    def receive(q, t):
        far[q * steps + t].wait_recv()
        own, other = own_rows(t), other_rows(t)
        forward = send(remote.at[q, own, :], remote.at[q, own, :], me_sibling)
        forwards.append(forward)
        index = used[-1]
        pltpu.make_async_remote_copy(
            src_ref=remote.at[q, other, :],
            dst_ref=remote.at[q, other, :],
            send_sem=send_sem.at[index],
            recv_sem=recv_sem.at[index],
            device_id=me_sibling,
            device_id_type=MESH,
        ).wait_recv()

    def section_one_own(r, j):
        section_one(r, j, total[(0, *at(r, j))] + remote[(0, *at(r, j))], True)

    for t in range(steps):
        receive(0, t)
        over(section_one_own, t, last - 2 * t, 2)
    pack_cols(first, classes + 1, pack, 4, own_tiles)
    col_halo_one = send_cols(pack, 4)

    def carry_second(r, j):
        factors = [coef[(i, *at(r + 1, j))] for i in range(5)]
        for k in range(classes):
            value = tile(field, k, r, j) + transported(first, k, r, j, factors)
            out[(k, *at(r, j))] = 0.5 * value
        moved[at(r, j)] = transported(first, classes, r, j, factors)

    over(carry_second, 0, 1, row_tiles, 1, 1, col_tiles - 2)
    for copy in col_halo_one:
        copy.wait_recv()
    unpack_cols(first, classes + 1, pack, 4, own_tiles, ())
    over(carry_second, 0, 1, row_tiles, 0, col_tiles - 1, 2)

    def finish(r, j):
        weighted = total[(1, *at(r, j))] + remote[(1, *at(r, j))]
        solids = moved[at(r, j)] - gain[at(r, j)] * weighted
        g = (0.5 * tile(field, classes + BED, r, j)) * hindered(solids)
        for k in range(classes):
            out[(k, *at(r, j))] = out[(k, *at(r, j))] - (speed[k] * g) * tile(first, k, r, j)

    for t in range(steps):
        receive(1, t)
        over(finish, t, last - 2 * t, 2)

    for copy in far + edge_sums + row_halo + col_halo + corners + forwards + col_halo_one:
        copy.wait_send()


def per_device(concentration, class_table, settle_speed, along_speed, across_speed, film_depth, cell_mask):
    classes, rows, cols = concentration.shape
    padded = (rows + 2 * SUB, cols + 2 * LANE)
    flat = (rows, cols)
    row_tiles = rows // SUB
    copies = 2 + 4 * (row_tiles // 2) + 4 + 4 + 6
    anywhere = pl.BlockSpec(memory_space=pl.ANY)
    f32 = jnp.float32

    def keep(array):
        return pltpu.with_memory_space_constraint(array, pltpu.HBM)

    return pl.pallas_call(
        section_kernel,
        out_shape=pltpu.VMEM(concentration.shape, f32),
        in_specs=[anywhere] * 7,
        out_specs=pl.BlockSpec(memory_space=pltpu.VMEM),
        scratch_shapes=[
            pltpu.SMEM(class_table.shape, jnp.int32),
            pltpu.SMEM(settle_speed.shape, f32),
            pltpu.VMEM((classes + 4, *padded), f32),
            pltpu.VMEM((classes + 1, *padded), f32),
            pltpu.VMEM((2, 2, SUB, cols), f32),
            pltpu.VMEM((2, *flat), f32),
            pltpu.VMEM((2, *flat), f32),
            pltpu.VMEM((2, *flat), f32),
            pltpu.VMEM((2, *flat), f32),
            pltpu.VMEM((5, rows + 2 * SUB, cols), f32),
            pltpu.VMEM(flat, f32),
            pltpu.VMEM(flat, f32),
            pltpu.VMEM(flat, f32),
            pltpu.VMEM(flat, jnp.int32),
            pltpu.VMEM((8, rows, LANE), f32),
            pltpu.VMEM((4, 2 * SUB, LANE), f32),
            pltpu.SemaphoreType.DMA((row_tiles + 6,)),
            pltpu.SemaphoreType.DMA((copies,)),
            pltpu.SemaphoreType.DMA((copies,)),
        ],
        compiler_params=pltpu.CompilerParams(
            collective_id=0, has_side_effects=True, vmem_limit_bytes=32 * 2**20
        ),
        cost_estimate=pl.CostEstimate(
            flops=40 * classes * rows * cols, bytes_accessed=8 * classes * rows * cols, transcendentals=4 * rows * cols
        ),
    )(*map(keep, (concentration, class_table, settle_speed, along_speed, across_speed, film_depth, cell_mask)))


def solution(mesh):
    grid = P("helix", "cross")
    return jax.shard_map(
        per_device,
        mesh=mesh,
        in_specs=(P("cls", "helix", "cross"), P("cls"), P(), grid, grid, grid, grid),
        out_specs=P("cls", "helix", "cross"),
        check_vma=False,
    )
```

time: 66.2 us -> 51.4 us (0.78)
  Pallas kernels: 58.1 us -> 49.9 us
  local copies, waits for them, and re-layouts: 7.84 us -> 1.32 us
    pallas_call x1, Pallas kernels: 58.1 us -> 49.9 us  [per_device(): pl.pallas_call(section_kernel, out_shape=pltpu.VMEM(concentration.shape,...]
    unnamed x15 -> x1, local copies, waits for them, and re-layouts: 7.84 us -> 1.32 us
where the time goes in v2:
time: 51.4 us; the launch traced here: 51.3 us
  Pallas kernels  49.9 us (97%)
  local copies, waits for them, and re-layouts  1.32 us (3%)
    pallas_call x1, Pallas kernels, per_device(): pl.pallas_call(section_kernel, out_shape=pltpu.VMEM(concentration.shape,...  49.9 us
    unnamed x1, local copies, waits for them, and re-layouts  1.32 us

profile of v2, /device:TPU:1, one launch (start us, length us, event | category | flops | bytes accessed | tf_op | source)
XLA Modules:
  0.0 51.3 jit_solution(2304151666789407043)
XLA Ops:
  0.0 49.9 %shard_map.73 = f32[16,32,1024]{2,1,0:T(8,128)S(1)} custom-call(f32[16,32,1024]{2,1,0:T(8,128)} %conc.1, s32[16]{0:T(128)} %table.1, f32[64]{0:T(128)} %settle.1, f32[32,1024]{1,0:T(8,128)} %along.1, f32[32,1024]{1,0:T(8,128)} %across.1, f32[32,1024]{1,0:T(8,128)} %depth.1, s32[32,1024]{1,0:T(8,128)} %mask.1), custom_call_target="tpu_custom_call" | custom-call | flops 20971520 | bytes 4194304 | tf_op jit(solution)/shard_map/pallas_call | solution.py:407
  49.9 1.3 %copy.9 = f32[16,32,1024]{2,1,0:T(8,128)} copy(f32[16,32,1024]{2,1,0:T(8,128)S(1)} %shard_map.73) | data formatting | bytes 4194304

commit v3 on v2

--- a/solution.py
+++ b/solution.py
@@ -62,6 +62,9 @@
     me_left = (helix, (cross + n_cross - 1) % n_cross, cls)
     me_right = (helix, (cross + 1) % n_cross, cls)
 
+    prev_left, prev_right = (me_prev[0], me_left[1], cls), (me_prev[0], me_right[1], cls)
+    next_left, next_right = (me_next[0], me_left[1], cls), (me_next[0], me_right[1], cls)
+
     inner_cols = pl.ds(LANE, cols)
     last = row_tiles - 1
     steps = row_tiles // 2
@@ -91,6 +94,7 @@
 
     barrier = pltpu.get_barrier_semaphore()
     peers = (me_sibling, me_partner, me_prev, me_next, far_prev, far_next, me_left, me_right)
+    peers += (prev_left, prev_right, next_left, next_right)
     for peer in peers:
         pl.semaphore_signal(barrier, inc=1, device_id=peer, device_id_type=MESH)
 
@@ -147,6 +151,34 @@
     for r in range(row_tiles):
         loads[r].wait()
         over(sums, r, 1, 1, unroll=2)
+
+    for copy in statics:
+        copy.wait()
+
+    def statics_of(r, j):
+        kind = mask_v[at(r, j)]
+        put(field, classes + WETTED, r, j, (kind > 0).astype(jnp.float32))
+        put(field, classes + BED, r, j, jnp.where(kind == 2, TIME_STEP, 0.0) / depth_v[at(r, j)])
+
+    over(statics_of, 0, 1, row_tiles)
+
+    def pack_cols(ref, count, dst, slot, tile_rows):
+        for i, r in enumerate(tile_rows):
+            head = jnp.zeros((SUB, LANE), jnp.float32)
+            tail = jnp.zeros((SUB, LANE), jnp.float32)
+            for p in range(count):
+                x = tile(ref, p, r, 0)
+                head = jnp.where(lane == p, pltpu.roll(x, p, 1) if p else x, head)
+                x = tile(ref, p, r, col_tiles - 1)
+                tail = jnp.where(lane == p, pltpu.roll(x, p + 1, 1), tail)
+            dst[(slot, *at(i, 0))] = head
+            dst[(slot + 1, *at(i, 0))] = tail
+
+    own_tiles = tuple(range(row_tiles))
+    outer_tiles = (-1, row_tiles)
+    walls = (classes + WETTED,)
+
+    pack_cols(field, classes + 3, pack, 0, own_tiles)
 
     used = []
 
@@ -183,16 +215,23 @@
             ),
         ]
 
-    row_halo = send_rows(0, classes)
+    def send_cols(src, slot):
+        return [
+            send(src.at[slot], src.at[slot + 2], me_left),
+            send(src.at[slot + 1], src.at[slot + 3], me_right),
+        ]
+
     shares.append(send(partial.at[1], sibling.at[1], me_sibling))
-
-    for copy in statics:
-        copy.wait()
-
-    def statics_of(r, j):
-        kind = mask_v[at(r, j)]
-        put(field, classes + WETTED, r, j, (kind > 0).astype(jnp.float32))
-        put(field, classes + BED, r, j, jnp.where(kind == 2, TIME_STEP, 0.0) / depth_v[at(r, j)])
+    col_halo = send_cols(pack, 0)
+    row_halo = send_rows(0, planes)
+    head_tile, tail_tile = pl.ds(0, SUB), pl.ds(rows - SUB, SUB)
+    upper, lower = pl.ds(0, SUB), pl.ds(SUB, SUB)
+    corners = [
+        send(pack.at[1, tail_tile], corner.at[1, upper], next_right),
+        send(pack.at[1, head_tile], corner.at[1, lower], prev_right),
+        send(pack.at[0, tail_tile], corner.at[0, upper], next_left),
+        send(pack.at[0, head_tile], corner.at[0, lower], prev_left),
+    ]
 
     def own_rows(t):
         return pl.ds(pl.multiple_of(SUB * (t + core * (last - 2 * t)), SUB), SUB)
@@ -220,31 +259,10 @@
         )
         edge_sums.append(send(total.at[0, pl.ds(0, 1), :], edges.at[source, 1, pl.ds(0, 1), :], before))
 
-    over(statics_of, 0, 1, row_tiles)
-    row_halo += send_rows(classes, 4)
-
-    def pack_cols(ref, count, dst, slot, tile_rows):
-        for i, r in enumerate(tile_rows):
-            head = jnp.zeros((SUB, LANE), jnp.float32)
-            tail = jnp.zeros((SUB, LANE), jnp.float32)
-            for p in range(count):
-                x = tile(ref, p, r, 0)
-                head = jnp.where(lane == p, pltpu.roll(x, p, 1) if p else x, head)
-                x = tile(ref, p, r, col_tiles - 1)
-                tail = jnp.where(lane == p, pltpu.roll(x, p + 1, 1), tail)
-            dst[(slot, *at(i, 0))] = head
-            dst[(slot + 1, *at(i, 0))] = tail
-
-    def send_cols(src, slot):
-        return [
-            send(src.at[slot], src.at[slot + 2], me_left),
-            send(src.at[slot + 1], src.at[slot + 3], me_right),
-        ]
-
     def unpack_cols(ref, count, src, slot, tile_rows, walls):
         for i, r in enumerate(tile_rows):
-            head = src[(slot + 2, *at(i, 0))]
-            tail = src[(slot + 3, *at(i, 0))]
+            head = src[(slot, *at(i, 0))]
+            tail = src[(slot + 1, *at(i, 0))]
             for p in range(count):
                 right = pltpu.roll(head, LANE - p, 1) if p else head
                 left = pltpu.roll(tail, LANE - 1 - p, 1)
@@ -254,12 +272,6 @@
                 put(ref, p, r, col_tiles, right)
                 put(ref, p, r, -1, left)
 
-    own_tiles = tuple(range(row_tiles))
-    outer_tiles = (-1, row_tiles)
-    walls = (classes + WETTED,)
-
-    pack_cols(field, classes + 3, pack, 0, own_tiles)
-    col_halo = send_cols(pack, 0)
     chip_sums(1)
 
     def coefficients(r, j, side=0):
@@ -301,21 +313,15 @@
         for k in range(classes):
             put(first, k, r, j, transported(field, k, r, j, factors, side))
 
+    def both_first(r, j):
+        coefficients(r, j)
+        carry_first(r, j)
+
+    over(both_first, 1, 1, row_tiles - 2, 1, 1, col_tiles - 2)
     for copy in col_halo:
         copy.wait_recv()
-    unpack_cols(field, classes + 3, pack, 0, own_tiles, walls)
-    over(coefficients, 1, 1, row_tiles - 2)
-    over(carry_first, 1, 1, row_tiles - 2)
-
-    for copy in row_halo:
-        copy.wait_recv()
-    pack_cols(field, classes + 3, corner, 0, outer_tiles)
-    corners = send_cols(corner, 0)
-    over(coefficients, 0, last, 2)
-    over(carry_first, 0, last, 2)
-    for copy in corners:
-        copy.wait_recv()
-    unpack_cols(field, classes + 3, corner, 0, outer_tiles, walls)
+    unpack_cols(field, classes + 3, pack, 2, own_tiles, walls)
+    over(both_first, 1, 1, row_tiles - 2, 0, col_tiles - 1, 2)
 
     def section_one(r, j, solids, keep_gain):
         put(first, classes, r, j, solids)
@@ -325,8 +331,45 @@
         for k in range(classes):
             put(first, k, r, j, tile(first, k, r, j) - (speed[k] * g) * tile(field, k, r, j))
 
-    for copy in edge_sums:
+    forwards = []
+
+    def forward(q):
+        sent = []
+        for t in range(steps):
+            far[q * steps + t].wait_recv()
+            own = own_rows(t)
+            sent.append((send(remote.at[q, own, :], remote.at[q, own, :], me_sibling), used[-1], t))
+        forwards.extend(copy for copy, _, _ in sent)
+        return sent
+
+    def arrived(q, sent):
+        for _, index, t in sent:
+            other = other_rows(t)
+            pltpu.make_async_remote_copy(
+                src_ref=remote.at[q, other, :],
+                dst_ref=remote.at[q, other, :],
+                send_sem=send_sem.at[index],
+                recv_sem=recv_sem.at[index],
+                device_id=me_sibling,
+                device_id_type=MESH,
+            ).wait_recv()
+
+    solids_sent = forward(0)
+    for copy in row_halo:
         copy.wait_recv()
+    over(both_first, 0, last, 2)
+    arrived(0, solids_sent)
+
+    def section_one_own(r, j):
+        section_one(r, j, total[(0, *at(r, j))] + remote[(0, *at(r, j))], True)
+
+    over(section_one_own, 0, 1, row_tiles)
+    pack_cols(first, classes + 1, pack, 4, own_tiles)
+    col_halo_one = send_cols(pack, 4)
+
+    for copy in edge_sums + corners:
+        copy.wait_recv()
+    unpack_cols(field, classes + 3, corner, 0, outer_tiles, walls)
     for side, r in ((-1, -1), (1, row_tiles)):
 
         def outer(_, j, side=side, r=r):
@@ -338,32 +381,6 @@
 
         over(outer, r, 1, 1, unroll=2)
 
-    forwards = []
-
-    def receive(q, t):
-        far[q * steps + t].wait_recv()
-        own, other = own_rows(t), other_rows(t)
-        forward = send(remote.at[q, own, :], remote.at[q, own, :], me_sibling)
-        forwards.append(forward)
-        index = used[-1]
-        pltpu.make_async_remote_copy(
-            src_ref=remote.at[q, other, :],
-            dst_ref=remote.at[q, other, :],
-            send_sem=send_sem.at[index],
-            recv_sem=recv_sem.at[index],
-            device_id=me_sibling,
-            device_id_type=MESH,
-        ).wait_recv()
-
-    def section_one_own(r, j):
-        section_one(r, j, total[(0, *at(r, j))] + remote[(0, *at(r, j))], True)
-
-    for t in range(steps):
-        receive(0, t)
-        over(section_one_own, t, last - 2 * t, 2)
-    pack_cols(first, classes + 1, pack, 4, own_tiles)
-    col_halo_one = send_cols(pack, 4)
-
     def carry_second(r, j):
         factors = [coef[(i, *at(r + 1, j))] for i in range(5)]
         for k in range(classes):
@@ -372,10 +389,12 @@
         moved[at(r, j)] = transported(first, classes, r, j, factors)
 
     over(carry_second, 0, 1, row_tiles, 1, 1, col_tiles - 2)
+    weighted_sent = forward(1)
     for copy in col_halo_one:
         copy.wait_recv()
-    unpack_cols(first, classes + 1, pack, 4, own_tiles, ())
+    unpack_cols(first, classes + 1, pack, 6, own_tiles, ())
     over(carry_second, 0, 1, row_tiles, 0, col_tiles - 1, 2)
+    arrived(1, weighted_sent)
 
     def finish(r, j):
         weighted = total[(1, *at(r, j))] + remote[(1, *at(r, j))]
@@ -384,9 +403,7 @@
         for k in range(classes):
             out[(k, *at(r, j))] = out[(k, *at(r, j))] - (speed[k] * g) * tile(first, k, r, j)
 
-    for t in range(steps):
-        receive(1, t)
-        over(finish, t, last - 2 * t, 2)
+    over(finish, 0, 1, row_tiles)
 
     for copy in far + edge_sums + row_halo + col_halo + corners + forwards + col_halo_one:
         copy.wait_send()
@@ -397,7 +414,7 @@
     padded = (rows + 2 * SUB, cols + 2 * LANE)
     flat = (rows, cols)
     row_tiles = rows // SUB
-    copies = 2 + 4 * (row_tiles // 2) + 4 + 4 + 6
+    copies = 2 + 4 * (row_tiles // 2) + 14
     anywhere = pl.BlockSpec(memory_space=pl.ANY)
     f32 = jnp.float32
 
@@ -425,7 +442,7 @@
             pltpu.VMEM(flat, f32),
             pltpu.VMEM(flat, jnp.int32),
             pltpu.VMEM((8, rows, LANE), f32),
-            pltpu.VMEM((4, 2 * SUB, LANE), f32),
+            pltpu.VMEM((2, 2 * SUB, LANE), f32),
             pltpu.SemaphoreType.DMA((row_tiles + 6,)),
             pltpu.SemaphoreType.DMA((copies,)),
             pltpu.SemaphoreType.DMA((copies,)),

time: 51.4 us -> 48 us (0.934)
  Pallas kernels: 49.9 us -> 46.5 us
    pallas_call x1, Pallas kernels: 49.9 us -> 46.5 us  [per_device(): pl.pallas_call(section_kernel, out_shape=pltpu.VMEM(concentration.shape,...]
where the time goes in v3:
time: 48 us; the launch traced here: 47.9 us
  Pallas kernels  46.5 us (97%)
  local copies, waits for them, and re-layouts  1.32 us (3%)
    pallas_call x1, Pallas kernels, per_device(): pl.pallas_call(section_kernel, out_shape=pltpu.VMEM(concentration.shape,...  46.5 us
    unnamed x1, local copies, waits for them, and re-layouts  1.32 us

profile of v3, /device:TPU:1, one launch (start us, length us, event | category | flops | bytes accessed | tf_op | source)
XLA Modules:
  0.0 47.9 jit_solution(10428809713314845948)
XLA Ops:
  0.0 46.5 %shard_map.73 = f32[16,32,1024]{2,1,0:T(8,128)S(1)} custom-call(f32[16,32,1024]{2,1,0:T(8,128)} %conc.1, s32[16]{0:T(128)} %table.1, f32[64]{0:T(128)} %settle.1, f32[32,1024]{1,0:T(8,128)} %along.1, f32[32,1024]{1,0:T(8,128)} %across.1, f32[32,1024]{1,0:T(8,128)} %depth.1, s32[32,1024]{1,0:T(8,128)} %mask.1), custom_call_target="tpu_custom_call" | custom-call | flops 20971520 | bytes 4194304 | tf_op jit(solution)/shard_map/pallas_call | solution.py:424
  46.5 1.3 %copy.9 = f32[16,32,1024]{2,1,0:T(8,128)} copy(f32[16,32,1024]{2,1,0:T(8,128)S(1)} %shard_map.73) | data formatting | bytes 4194304

commit v4 on v3

--- a/solution.py
+++ b/solution.py
@@ -47,6 +47,7 @@
     load_sem,
     send_sem,
     recv_sem,
+    ready_sem,
 ):
     classes, rows, cols = conc.shape
     row_tiles, col_tiles = rows // SUB, cols // LANE
@@ -93,10 +94,25 @@
         copy.start()
 
     barrier = pltpu.get_barrier_semaphore()
-    peers = (me_sibling, me_partner, me_prev, me_next, far_prev, far_next, me_left, me_right)
-    peers += (prev_left, prev_right, next_left, next_right)
-    for peer in peers:
+    rank = half * n_helix + helix
+    near_peers = (me_sibling, me_left, me_right)
+    far_peers = (
+        me_partner, me_prev, me_next, far_prev, far_next, prev_left, prev_right, next_left, next_right
+    )
+    inverse = (0, 2, 1, 4, 3, 8, 7, 6, 5)
+    PARTNER, PREV, NEXT, FAR_PREV, FAR_NEXT, PREV_LEFT, PREV_RIGHT, NEXT_LEFT, NEXT_RIGHT = range(9)
+    ranks = [peer[2] // 2 * n_helix + peer[0] for peer in far_peers]
+    higher = [other - rank > 1 for other in ranks]
+    lower = [rank - other > 1 for other in ranks]
+    expected = len(near_peers)
+    for peer in near_peers:
         pl.semaphore_signal(barrier, inc=1, device_id=peer, device_id_type=MESH)
+    for i, peer in enumerate(far_peers):
+        expected = expected + jnp.where(higher[i], 0, 1)
+
+        @pl.when(jnp.logical_not(lower[i]))
+        def _(peer=peer):
+            pl.semaphore_signal(barrier, inc=1, device_id=peer, device_id_type=MESH)
 
     for copy in scalars:
         copy.wait()
@@ -182,7 +198,10 @@
 
     used = []
 
-    def send(src, dst, peer):
+    held = [[] for _ in far_peers]
+
+    def send(src, dst, peer, relation=None):
+        peer = peer if relation is None else far_peers[relation]
         index = len(used)
         used.append(index)
         copy = pltpu.make_async_remote_copy(
@@ -193,10 +212,28 @@
             device_id=peer,
             device_id_type=MESH,
         )
-        copy.start()
+        if relation is None:
+            copy.start()
+        else:
+            pl.when(jnp.logical_not(higher[relation]))(copy.start)
+            held[relation].append(copy)
         return copy
 
-    pl.semaphore_wait(barrier, len(peers))
+    def release():
+        for i, copies in enumerate(held):
+
+            @pl.when(higher[i])
+            def _(i=i, copies=copies):
+                pl.semaphore_wait(ready_sem.at[i], 1)
+                for copy in copies:
+                    copy.start()
+
+    pl.semaphore_wait(barrier, expected)
+    for i, peer in enumerate(far_peers):
+
+        @pl.when(lower[i])
+        def _(i=i, peer=peer):
+            pl.semaphore_signal(ready_sem.at[inverse[i]], inc=1, device_id=peer, device_id_type=MESH)
 
     shares = [send(partial.at[0], sibling.at[0], me_sibling)]
 
@@ -206,12 +243,14 @@
             send(
                 field.at[some, pl.ds(SUB + rows - 2, 2), inner_cols],
                 field.at[some, pl.ds(SUB - 2, 2), inner_cols],
-                me_next,
+                None,
+                NEXT,
             ),
             send(
                 field.at[some, pl.ds(SUB, 2), inner_cols],
                 field.at[some, pl.ds(SUB + rows, 2), inner_cols],
-                me_prev,
+                None,
+                PREV,
             ),
         ]
 
@@ -227,10 +266,10 @@
     head_tile, tail_tile = pl.ds(0, SUB), pl.ds(rows - SUB, SUB)
     upper, lower = pl.ds(0, SUB), pl.ds(SUB, SUB)
     corners = [
-        send(pack.at[1, tail_tile], corner.at[1, upper], next_right),
-        send(pack.at[1, head_tile], corner.at[1, lower], prev_right),
-        send(pack.at[0, tail_tile], corner.at[0, upper], next_left),
-        send(pack.at[0, head_tile], corner.at[0, lower], prev_left),
+        send(pack.at[1, tail_tile], corner.at[1, upper], None, NEXT_RIGHT),
+        send(pack.at[1, head_tile], corner.at[1, lower], None, PREV_RIGHT),
+        send(pack.at[0, tail_tile], corner.at[0, upper], None, NEXT_LEFT),
+        send(pack.at[0, head_tile], corner.at[0, lower], None, PREV_LEFT),
     ]
 
     def own_rows(t):
@@ -246,18 +285,18 @@
         for t in range(steps):
             own = own_rows(t)
             total[q, own, :] = partial[q, own, :] + sibling[q, own, :]
-            far.append(send(total.at[q, own, :], remote.at[q, own, :], me_partner))
+            far.append(send(total.at[q, own, :], remote.at[q, own, :], None, PARTNER))
         for t in range(steps):
             other = other_rows(t)
             total[q, other, :] = partial[q, other, :] + sibling[q, other, :]
 
     chip_sums(0)
     edge_sums = []
-    for source, after, before in ((0, me_next, me_prev), (1, far_next, far_prev)):
+    for source, after, before in ((0, NEXT, PREV), (1, FAR_NEXT, FAR_PREV)):
         edge_sums.append(
-            send(total.at[0, pl.ds(rows - 1, 1), :], edges.at[source, 0, pl.ds(SUB - 1, 1), :], after)
+            send(total.at[0, pl.ds(rows - 1, 1), :], edges.at[source, 0, pl.ds(SUB - 1, 1), :], None, after)
         )
-        edge_sums.append(send(total.at[0, pl.ds(0, 1), :], edges.at[source, 1, pl.ds(0, 1), :], before))
+        edge_sums.append(send(total.at[0, pl.ds(0, 1), :], edges.at[source, 1, pl.ds(0, 1), :], None, before))
 
     def unpack_cols(ref, count, src, slot, tile_rows, walls):
         for i, r in enumerate(tile_rows):
@@ -354,10 +393,11 @@
                 device_id_type=MESH,
             ).wait_recv()
 
-    solids_sent = forward(0)
+    release()
     for copy in row_halo:
         copy.wait_recv()
     over(both_first, 0, last, 2)
+    solids_sent = forward(0)
     arrived(0, solids_sent)
 
     def section_one_own(r, j):
@@ -446,6 +486,7 @@
             pltpu.SemaphoreType.DMA((row_tiles + 6,)),
             pltpu.SemaphoreType.DMA((copies,)),
             pltpu.SemaphoreType.DMA((copies,)),
+            pltpu.SemaphoreType.REGULAR((9,)),
         ],
         compiler_params=pltpu.CompilerParams(
             collective_id=0, has_side_effects=True, vmem_limit_bytes=32 * 2**20

time: 48 us -> 42.2 us (0.88)
  the two profiles are of different devices: /device:TPU:1 before, /device:TPU:129 now
where the time goes in v4:
time: 42.2 us; the launch traced here: 42.1 us
  Pallas kernels  40.7 us (96%)
  local copies, waits for them, and re-layouts  1.32 us (3%)
    pallas_call x1, Pallas kernels, per_device(): pl.pallas_call(section_kernel, out_shape=pltpu.VMEM(concentration.shape,...  40.7 us
    unnamed x1, local copies, waits for them, and re-layouts  1.32 us

profile of v4, /device:TPU:129, one launch (start us, length us, event | category | flops | bytes accessed | tf_op | source)
XLA Modules:
  0.0 42.1 jit_solution(12452189792748384204)
XLA Ops:
  0.0 40.7 %shard_map.73 = f32[16,32,1024]{2,1,0:T(8,128)S(1)} custom-call(f32[16,32,1024]{2,1,0:T(8,128)} %conc.1, s32[16]{0:T(128)} %table.1, f32[64]{0:T(128)} %settle.1, f32[32,1024]{1,0:T(8,128)} %along.1, f32[32,1024]{1,0:T(8,128)} %across.1, f32[32,1024]{1,0:T(8,128)} %depth.1, s32[32,1024]{1,0:T(8,128)} %mask.1), custom_call_target="tpu_custom_call" | custom-call | flops 20971520 | bytes 4194304 | tf_op jit(solution)/shard_map/pallas_call | solution.py:464
  40.7 1.3 %copy.9 = f32[16,32,1024]{2,1,0:T(8,128)} copy(f32[16,32,1024]{2,1,0:T(8,128)S(1)} %shard_map.73) | data formatting | bytes 4194304

commit v5 on v4

--- a/solution.py
+++ b/solution.py
@@ -94,16 +94,17 @@
         copy.start()
 
     barrier = pltpu.get_barrier_semaphore()
-    rank = half * n_helix + helix
-    near_peers = (me_sibling, me_left, me_right)
+    rank = (half * n_helix + helix) * n_cross + cross
+    near_peers = (me_sibling,)
     far_peers = (
-        me_partner, me_prev, me_next, far_prev, far_next, prev_left, prev_right, next_left, next_right
+        me_partner, me_prev, me_next, far_prev, far_next, prev_left, prev_right, next_left, next_right, me_left, me_right
     )
-    inverse = (0, 2, 1, 4, 3, 8, 7, 6, 5)
-    PARTNER, PREV, NEXT, FAR_PREV, FAR_NEXT, PREV_LEFT, PREV_RIGHT, NEXT_LEFT, NEXT_RIGHT = range(9)
-    ranks = [peer[2] // 2 * n_helix + peer[0] for peer in far_peers]
-    higher = [other - rank > 1 for other in ranks]
-    lower = [rank - other > 1 for other in ranks]
+    inverse = (0, 2, 1, 4, 3, 8, 7, 6, 5, 10, 9)
+    PARTNER, PREV, NEXT, FAR_PREV, FAR_NEXT, PREV_LEFT, PREV_RIGHT, NEXT_LEFT, NEXT_RIGHT, LEFT, RIGHT = range(11)
+    ranks = [(peer[2] // 2 * n_helix + peer[0]) * n_cross + peer[1] for peer in far_peers]
+    higher = [other > rank for other in ranks]
+    lower = [other < rank for other in ranks]
+    close = [jnp.abs(other - rank) <= 2 * n_cross for other in ranks]
     expected = len(near_peers)
     for peer in near_peers:
         pl.semaphore_signal(barrier, inc=1, device_id=peer, device_id_type=MESH)
@@ -168,16 +169,6 @@
         loads[r].wait()
         over(sums, r, 1, 1, unroll=2)
 
-    for copy in statics:
-        copy.wait()
-
-    def statics_of(r, j):
-        kind = mask_v[at(r, j)]
-        put(field, classes + WETTED, r, j, (kind > 0).astype(jnp.float32))
-        put(field, classes + BED, r, j, jnp.where(kind == 2, TIME_STEP, 0.0) / depth_v[at(r, j)])
-
-    over(statics_of, 0, 1, row_tiles)
-
     def pack_cols(ref, count, dst, slot, tile_rows):
         for i, r in enumerate(tile_rows):
             head = jnp.zeros((SUB, LANE), jnp.float32)
@@ -194,13 +185,14 @@
     outer_tiles = (-1, row_tiles)
     walls = (classes + WETTED,)
 
-    pack_cols(field, classes + 3, pack, 0, own_tiles)
-
     used = []
 
     held = [[] for _ in far_peers]
-
-    def send(src, dst, peer, relation=None):
+    held_last = []
+    calm = jnp.logical_and(half == 1, jnp.logical_and(8 * helix >= 2 * n_helix, 8 * helix < 4 * n_helix))
+    patient = jnp.logical_and(half == 1, 8 * helix >= 5 * n_helix)
+
+    def send(src, dst, peer, relation=None, later=False):
         peer = peer if relation is None else far_peers[relation]
         index = len(used)
         used.append(index)
@@ -215,14 +207,17 @@
         if relation is None:
             copy.start()
         else:
-            pl.when(jnp.logical_not(higher[relation]))(copy.start)
-            held[relation].append(copy)
+            now = jnp.logical_not(higher[relation])
+            if later:
+                now = jnp.logical_and(now, jnp.logical_not(jnp.logical_or(patient, calm)))
+            pl.when(now)(copy.start)
+            (held_last if later else held[relation]).append(copy)
         return copy
 
-    def release():
+    def release(near):
         for i, copies in enumerate(held):
 
-            @pl.when(higher[i])
+            @pl.when(jnp.logical_and(higher[i], close[i] if near else jnp.logical_not(close[i])))
             def _(i=i, copies=copies):
                 pl.semaphore_wait(ready_sem.at[i], 1)
                 for copy in copies:
@@ -254,14 +249,26 @@
             ),
         ]
 
-    def send_cols(src, slot):
+    def send_cols(src, slot, left, right):
         return [
-            send(src.at[slot], src.at[slot + 2], me_left),
-            send(src.at[slot + 1], src.at[slot + 3], me_right),
+            send(src.at[slot], src.at[slot + 2], me_left, left),
+            send(src.at[slot + 1], src.at[slot + 3], me_right, right),
         ]
 
     shares.append(send(partial.at[1], sibling.at[1], me_sibling))
-    col_halo = send_cols(pack, 0)
+    for copy in statics:
+        copy.wait()
+
+    def statics_of(r, j):
+        kind = mask_v[at(r, j)]
+        put(field, classes + WETTED, r, j, (kind > 0).astype(jnp.float32))
+        put(field, classes + BED, r, j, jnp.where(kind == 2, TIME_STEP, 0.0) / depth_v[at(r, j)])
+
+    over(statics_of, 0, 1, row_tiles)
+
+    pack_cols(field, classes + 3, pack, 0, own_tiles)
+
+    col_halo = send_cols(pack, 0, LEFT, RIGHT)
     row_halo = send_rows(0, planes)
     head_tile, tail_tile = pl.ds(0, SUB), pl.ds(rows - SUB, SUB)
     upper, lower = pl.ds(0, SUB), pl.ds(SUB, SUB)
@@ -285,7 +292,7 @@
         for t in range(steps):
             own = own_rows(t)
             total[q, own, :] = partial[q, own, :] + sibling[q, own, :]
-            far.append(send(total.at[q, own, :], remote.at[q, own, :], None, PARTNER))
+            far.append(send(total.at[q, own, :], remote.at[q, own, :], None, PARTNER, q == 1))
         for t in range(steps):
             other = other_rows(t)
             total[q, other, :] = partial[q, other, :] + sibling[q, other, :]
@@ -357,6 +364,7 @@
         carry_first(r, j)
 
     over(both_first, 1, 1, row_tiles - 2, 1, 1, col_tiles - 2)
+    release(True)
     for copy in col_halo:
         copy.wait_recv()
     unpack_cols(field, classes + 3, pack, 2, own_tiles, walls)
@@ -393,11 +401,23 @@
                 device_id_type=MESH,
             ).wait_recv()
 
-    release()
+    release(False)
     for copy in row_halo:
         copy.wait_recv()
     over(both_first, 0, last, 2)
+
+    @pl.when(calm)
+    def _():
+        for copy in held_last:
+            copy.start()
+
     solids_sent = forward(0)
+
+    @pl.when(jnp.logical_or(higher[PARTNER], patient))
+    def _():
+        for copy in held_last:
+            copy.start()
+
     arrived(0, solids_sent)
 
     def section_one_own(r, j):
@@ -405,7 +425,7 @@
 
     over(section_one_own, 0, 1, row_tiles)
     pack_cols(first, classes + 1, pack, 4, own_tiles)
-    col_halo_one = send_cols(pack, 4)
+    col_halo_one = send_cols(pack, 4, None, None)
 
     for copy in edge_sums + corners:
         copy.wait_recv()
@@ -486,7 +506,7 @@
             pltpu.SemaphoreType.DMA((row_tiles + 6,)),
             pltpu.SemaphoreType.DMA((copies,)),
             pltpu.SemaphoreType.DMA((copies,)),
-            pltpu.SemaphoreType.REGULAR((9,)),
+            pltpu.SemaphoreType.REGULAR((11,)),
         ],
         compiler_params=pltpu.CompilerParams(
             collective_id=0, has_side_effects=True, vmem_limit_bytes=32 * 2**20

time: 42.2 us -> 40.6 us (0.962)
  the two profiles are of different devices: /device:TPU:129 before, /device:TPU:65 now
where the time goes in v5:
time: 40.6 us; the launch traced here: 40.4 us
  Pallas kernels  39.1 us (96%)
  local copies, waits for them, and re-layouts  1.32 us (3%)
    pallas_call x1, Pallas kernels, per_device(): pl.pallas_call(section_kernel, out_shape=pltpu.VMEM(concentration.shape,...  39.1 us
    unnamed x1, local copies, waits for them, and re-layouts  1.32 us

profile of v5, /device:TPU:65, one launch (start us, length us, event | category | flops | bytes accessed | tf_op | source)
XLA Modules:
  0.0 40.4 jit_solution(12297411898215123613)
XLA Ops:
  0.0 39.1 %shard_map.73 = f32[16,32,1024]{2,1,0:T(8,128)S(1)} custom-call(f32[16,32,1024]{2,1,0:T(8,128)} %conc.1, s32[16]{0:T(128)} %table.1, f32[64]{0:T(128)} %settle.1, f32[32,1024]{1,0:T(8,128)} %along.1, f32[32,1024]{1,0:T(8,128)} %across.1, f32[32,1024]{1,0:T(8,128)} %depth.1, s32[32,1024]{1,0:T(8,128)} %mask.1), custom_call_target="tpu_custom_call" | custom-call | flops 20971520 | bytes 4194304 | tf_op jit(solution)/shard_map/pallas_call | solution.py:484
  39.1 1.3 %copy.9 = f32[16,32,1024]{2,1,0:T(8,128)} copy(f32[16,32,1024]{2,1,0:T(8,128)S(1)} %shard_map.73) | data formatting | bytes 4194304

commit v6 on v5

--- a/solution.py
+++ b/solution.py
@@ -167,7 +167,7 @@
 
     for r in range(row_tiles):
         loads[r].wait()
-        over(sums, r, 1, 1, unroll=2)
+        over(sums, r, 1, 1, unroll=4)
 
     def pack_cols(ref, count, dst, slot, tile_rows):
         for i, r in enumerate(tile_rows):
@@ -423,7 +423,7 @@
     def section_one_own(r, j):
         section_one(r, j, total[(0, *at(r, j))] + remote[(0, *at(r, j))], True)
 
-    over(section_one_own, 0, 1, row_tiles)
+    over(section_one_own, 0, 1, row_tiles, unroll=8)
     pack_cols(first, classes + 1, pack, 4, own_tiles)
     col_halo_one = send_cols(pack, 4, None, None)
 
@@ -463,7 +463,7 @@
         for k in range(classes):
             out[(k, *at(r, j))] = out[(k, *at(r, j))] - (speed[k] * g) * tile(first, k, r, j)
 
-    over(finish, 0, 1, row_tiles)
+    over(finish, 0, 1, row_tiles, unroll=8)
 
     for copy in far + edge_sums + row_halo + col_halo + corners + forwards + col_halo_one:
         copy.wait_send()

time: 40.6 us -> 40.5 us (level)
  no operation moved by 1% of the time
where the time goes in v6:
time: 40.5 us; the launch traced here: 40.3 us
  Pallas kernels  39 us (96%)
  local copies, waits for them, and re-layouts  1.32 us (3%)
    pallas_call x1, Pallas kernels, per_device(): pl.pallas_call(section_kernel, out_shape=pltpu.VMEM(concentration.shape,...  39 us
    unnamed x1, local copies, waits for them, and re-layouts  1.32 us

profile of v6, /device:TPU:65, one launch (start us, length us, event | category | flops | bytes accessed | tf_op | source)
XLA Modules:
  0.0 40.3 jit_solution(2825673303352701959)
XLA Ops:
  0.0 39.0 %shard_map.73 = f32[16,32,1024]{2,1,0:T(8,128)S(1)} custom-call(f32[16,32,1024]{2,1,0:T(8,128)} %conc.1, s32[16]{0:T(128)} %table.1, f32[64]{0:T(128)} %settle.1, f32[32,1024]{1,0:T(8,128)} %along.1, f32[32,1024]{1,0:T(8,128)} %across.1, f32[32,1024]{1,0:T(8,128)} %depth.1, s32[32,1024]{1,0:T(8,128)} %mask.1), custom_call_target="tpu_custom_call" | custom-call | flops 20971520 | bytes 4194304 | tf_op jit(solution)/shard_map/pallas_call | solution.py:484
  39.0 1.3 %copy.9 = f32[16,32,1024]{2,1,0:T(8,128)} copy(f32[16,32,1024]{2,1,0:T(8,128)S(1)} %shard_map.73) | data formatting | bytes 4194304
